TPU v7x, 32 devices: a whole 2x2x4 slice. The times are simulated.
32 devices in a mesh: dp: 16 (over z, y, x), blk: 2 (over core).
Axes of the slice: x: 2, y: 2, z: 4, core: 2. Of those that a mesh axis runs over, the one named last changes fastest.
Arguments:
- hidden_in: bfloat16 [16, 512, 768], P('dp', 'blk'), may hold values from -6 to 6
- project_weight: bfloat16 [768, 2304], replicated, may hold values from -0.21875 to 0.21875
- output_weight: bfloat16 [768, 768], replicated, may hold values from -1.25 to 1.25
- expand_weight: bfloat16 [768, 3072], replicated, may hold values from -0.21875 to 0.21875
- reduce_weight: bfloat16 [3072, 768], replicated, may hold values from -0.109375 to 0.109375
- query_bias: float32 [768], replicated, may hold values from -3 to 3
- value_bias: float32 [768], replicated, may hold values from -3 to 3
- output_bias: float32 [768], replicated, may hold values from -3 to 3
- first_gain: float32 [768], replicated, may hold values from 0.5 to 1.5
- first_shift: float32 [768], replicated, may hold values from -3 to 3
- expand_bias: float32 [3072], replicated, may hold values from -3 to 3
- reduce_bias: float32 [768], replicated, may hold values from -3 to 3
- second_gain: float32 [768], replicated, may hold values from 0.5 to 1.5
- second_shift: float32 [768], replicated, may hold values from -3 to 3
- upstream: bfloat16 [16, 512, 768], P('dp', 'blk'), may hold values from -6 to 6
- teacher_maps: bfloat16 [16, 12, 512, 512], P('dp', None, 'blk'), may hold values from 0.5 to 8
- start_vector: float32 [768], replicated, may hold values from -5 to 5
- end_vector: float32 [768], replicated, may hold values from -5 to 5
- valid_length: int32 [16], P('dp'), may hold values from 257 to 512, as said below
- start_index: int32 [16], P('dp'), may hold values from 1 to 511, as said below
- end_index: int32 [16], P('dp'), may hold values from 1 to 511, as said below
- answerable: int32 [16], P('dp'), may hold values 0 or 1
Outputs:
- layer_output: bfloat16 [16, 512, 768], P('dp', 'blk')
- input_gradient: bfloat16 [16, 512, 768], P('dp', 'blk')
- weight_gradients: float32 [7087104], P(('dp', 'blk'))
Inputs may be any that keep to these rules, and one draw needn't show every extreme that they name: `valid_length`: tokens of a row at or beyond its length are padding; padding lies within a row's last 512 // 2 tokens; every fourth row, from the first, is at full length 512. start_index <= end_index < valid_length of the same row; full-length rows start at 511. start_index <= end_index < valid_length of the same row; full-length rows end at 511.
All inputs are finite; a program needn't handle non-finite values. No bound on the sum of `answerable` on one device may be relied on, other than what follows from the above.
Results may differ from a plain program's by a relative error of at most 0.014.
Values may be sent and summed in bfloat16 or wider, within the bound.
A program may use at most 192 MiB of HBM per device.

v0:
```python
import jax
import jax.numpy as jnp
from jax import lax
from jax.sharding import PartitionSpec as P

HEADS = 12
HEAD_DIM = 64


norm_eps = 1e-12


def layer_norm(field_in, gain_vec, shift_vec):
    centre = field_in - jnp.mean(field_in, axis=-1, keepdims=True)
    spread = jnp.mean(centre * centre, axis=-1, keepdims=True)
    return centre * lax.rsqrt(spread + norm_eps) * gain_vec + shift_vec


def gelu_exact(field_in):
    return jax.nn.gelu(field_in, approximate=False)


def outer_sum(left, right):
    return jnp.einsum("nd,ne->de", left, right, preferred_element_type=jnp.float32)


def column_sum(values_low):
    return jnp.sum(values_low.astype(jnp.float32), axis=0)


def body(
    hidden_in,
    project_weight,
    output_weight,
    expand_weight,
    reduce_weight,
    query_bias,
    value_bias,
    output_bias,
    first_gain,
    first_shift,
    expand_bias,
    reduce_bias,
    second_gain,
    second_shift,
    upstream,
    teacher_maps,
    start_vector,
    end_vector,
    valid_length,
    start_index,
    end_index,
    answerable,
):
    row_count, block_len, width = hidden_in.shape
    blocks = lax.axis_size("blk")
    length = block_len * blocks
    offset = lax.axis_index("blk") * block_len
    token_count = row_count * block_len
    positions = offset + jnp.arange(block_len, dtype=jnp.int32)
    key_live = jnp.arange(length, dtype=jnp.int32)[None, :] < valid_length[:, None]
    row_live = positions[None, :] < valid_length[:, None]
    score_scale = HEAD_DIM ** (-0.5)
    tokens = hidden_in.reshape(token_count, width)
    joined_bias = jnp.concatenate([query_bias, jnp.zeros_like(query_bias), value_bias])
    project = (
        jnp.dot(tokens, project_weight, preferred_element_type=jnp.float32) + joined_bias
    ).astype(jnp.bfloat16)
    queries = project[:, :width].reshape(row_count, block_len, HEADS, HEAD_DIM)
    keys_own = project[:, width : 2 * width].reshape(row_count, block_len, width)
    values_own = project[:, 2 * width :].reshape(row_count, block_len, width)
    keys_all, values_all = (
        lax.all_gather(keys_own, "blk", axis=1, tiled=True),
        lax.all_gather(values_own, "blk", axis=1, tiled=True),
    )

    def scores_of(keys_full):
        raw = (
            jnp.einsum(
                "rqhe,rkhe->rhqk",
                queries,
                keys_full.reshape(row_count, length, HEADS, HEAD_DIM),
                preferred_element_type=jnp.float32,
            )
            * score_scale
        )
        return jnp.where(key_live[:, None, None, :], raw, -1e30)

    scores = scores_of(keys_all)
    row_peak = jnp.max(scores, axis=-1, keepdims=True)
    expo_terms = jnp.exp(scores - row_peak)
    row_total = jnp.sum(expo_terms, axis=-1, keepdims=True)
    soft_low = (expo_terms / row_total).astype(jnp.bfloat16)
    log_total = row_peak + jnp.log(row_total)
    attended = (
        jnp.einsum(
            "rhqk,rkhe->rqhe",
            soft_low,
            values_all.reshape(row_count, length, HEADS, HEAD_DIM),
            preferred_element_type=jnp.float32,
        )
        .reshape(token_count, width)
        .astype(jnp.bfloat16)
    )
    branch = jnp.dot(attended, output_weight, preferred_element_type=jnp.float32) + output_bias
    resid_one = tokens.astype(jnp.float32) + branch
    mixed, first_pull = jax.vjp(layer_norm, resid_one, first_gain, first_shift)
    mixed_low = mixed.astype(jnp.bfloat16)
    expanded = jnp.dot(mixed_low, expand_weight, preferred_element_type=jnp.float32) + expand_bias
    active, gelu_pull = jax.vjp(gelu_exact, expanded)
    active_low = active.astype(jnp.bfloat16)
    reduced = jnp.dot(active_low, reduce_weight, preferred_element_type=jnp.float32) + reduce_bias
    result, second_pull = jax.vjp(layer_norm, mixed + reduced, second_gain, second_shift)
    layer_output = result.astype(jnp.bfloat16).reshape(row_count, block_len, width)
    start_slot = jnp.where(answerable > 0, start_index, 0)
    end_slot = jnp.where(answerable > 0, end_index, 0)
    cotangent = (
        upstream.astype(jnp.float32) * row_live[..., None].astype(jnp.float32)
        + (positions[None, :] == start_slot[:, None])[..., None].astype(jnp.float32) * start_vector
        + (positions[None, :] == end_slot[:, None])[..., None].astype(jnp.float32) * end_vector
    )
    grad_resid_two, grad_second_gain, grad_second_shift = second_pull(
        cotangent.reshape(token_count, width)
    )
    grad_reduced = grad_resid_two.astype(jnp.bfloat16)
    grad_active = jnp.einsum(
        "nd,fd->nf", grad_reduced, reduce_weight, preferred_element_type=jnp.float32
    )
    grad_expanded = gelu_pull(grad_active)[0].astype(jnp.bfloat16)
    grad_mixed = grad_resid_two + jnp.einsum(
        "nf,df->nd", grad_expanded, expand_weight, preferred_element_type=jnp.float32
    )
    grad_resid_one, grad_first_gain, grad_first_shift = first_pull(grad_mixed)
    grad_branch = grad_resid_one.astype(jnp.bfloat16)
    grad_attended = jnp.einsum(
        "ne,de->nd", grad_branch, output_weight, preferred_element_type=jnp.float32
    )
    grad_attended = grad_attended.astype(jnp.bfloat16).reshape(
        row_count, block_len, HEADS, HEAD_DIM
    )
    keys_back, values_back = (
        lax.all_gather(keys_own, "blk", axis=1, tiled=True),
        lax.all_gather(values_own, "blk", axis=1, tiled=True),
    )
    keys_heads = keys_back.reshape(row_count, length, HEADS, HEAD_DIM)
    values_heads = values_back.reshape(row_count, length, HEADS, HEAD_DIM)
    soft = jnp.exp(scores_of(keys_back) - log_total)
    both_live = row_live[:, None, :, None] & key_live[:, None, None, :]
    teacher_live = jnp.where(both_live, teacher_maps.astype(jnp.float32), 0.0)
    teacher_total = jnp.sum(teacher_live, axis=-1, keepdims=True)
    grad_soft = jnp.einsum(
        "rqhe,rkhe->rhqk", grad_attended, values_heads, preferred_element_type=jnp.float32
    )
    row_delta = jnp.sum(grad_soft * soft, axis=-1, keepdims=True)
    grad_scores = (
        soft * (grad_soft - row_delta) + (teacher_total * soft - teacher_live) / length
    ).astype(jnp.bfloat16)
    grad_query = (
        jnp.einsum("rhqk,rkhe->rqhe", grad_scores, keys_heads, preferred_element_type=jnp.float32)
        * score_scale
    )
    grad_keys = (
        jnp.einsum(
            "rhqk,rqhe->rkhe", grad_scores, queries, preferred_element_type=jnp.float32
        ).reshape(row_count, length, width)
        * score_scale
    )
    grad_values = jnp.einsum(
        "rhqk,rqhe->rkhe", soft_low, grad_attended, preferred_element_type=jnp.float32
    ).reshape(row_count, length, width)
    keys_grad_own, values_grad_own = (
        lax.psum_scatter(
            grad_keys.astype(jnp.bfloat16), "blk", scatter_dimension=1, tiled=True
        ).astype(jnp.float32),
        lax.psum_scatter(
            grad_values.astype(jnp.bfloat16), "blk", scatter_dimension=1, tiled=True
        ).astype(jnp.float32),
    )
    grad_project = jnp.concatenate(
        [
            grad_query.reshape(token_count, width),
            keys_grad_own.reshape(token_count, width),
            values_grad_own.reshape(token_count, width),
        ],
        axis=1,
    ).astype(jnp.bfloat16)
    grad_input = grad_resid_one + jnp.einsum(
        "ne,de->nd", grad_project, project_weight, preferred_element_type=jnp.float32
    )
    input_gradient = grad_input.astype(jnp.bfloat16).reshape(row_count, block_len, width)
    (
        tokens_both,
        project_both,
        attended_both,
        branch_both,
        mixed_both,
        expanded_both,
        active_both,
        reduced_both,
    ) = (
        lax.all_gather(tokens, "blk", axis=0, tiled=True),
        lax.all_gather(grad_project, "blk", axis=0, tiled=True),
        lax.all_gather(attended, "blk", axis=0, tiled=True),
        lax.all_gather(grad_branch, "blk", axis=0, tiled=True),
        lax.all_gather(mixed_low, "blk", axis=0, tiled=True),
        lax.all_gather(grad_expanded, "blk", axis=0, tiled=True),
        lax.all_gather(active_low, "blk", axis=0, tiled=True),
        lax.all_gather(grad_reduced, "blk", axis=0, tiled=True),
    )
    project_sums = column_sum(project_both)
    norm_grads = lax.psum(
        (grad_first_gain, grad_first_shift, grad_second_gain, grad_second_shift), "blk"
    )
    flat_grads = jnp.concatenate(
        [
            outer_sum(tokens_both, project_both).reshape(-1),
            outer_sum(attended_both, branch_both).reshape(-1),
            outer_sum(mixed_both, expanded_both).reshape(-1),
            outer_sum(active_both, reduced_both).reshape(-1),
            project_sums[:width],
            project_sums[2 * width :],
            column_sum(branch_both),
            norm_grads[0],
            norm_grads[1],
            column_sum(expanded_both),
            column_sum(reduced_both),
            norm_grads[2],
            norm_grads[3],
        ]
    )
    data_count = lax.axis_size("dp")
    piece_len = flat_grads.shape[0] // (data_count * blocks)
    mine = lax.dynamic_index_in_dim(
        flat_grads.reshape(data_count, blocks, piece_len), lax.axis_index("blk"), 1, keepdims=False
    )
    weight_gradients = lax.psum_scatter(mine, "dp", scatter_dimension=0, tiled=True).reshape(
        piece_len
    )
    return (layer_output, input_gradient, weight_gradients)


def solution(mesh):
    placed = (
        P("dp", "blk", None),
        P(),
        P(),
        P(),
        P(),
        P(),
        P(),
        P(),
        P(),
        P(),
        P(),
        P(),
        P(),
        P(),
        P("dp", "blk", None),
        P("dp", None, "blk", None),
        P(),
        P(),
        P("dp"),
        P("dp"),
        P("dp"),
        P("dp"),
    )
    return jax.shard_map(
        body,
        mesh=mesh,
        in_specs=placed,
        out_specs=(P("dp", "blk", None), P("dp", "blk", None), P(("dp", "blk"))),
        check_vma=False,
    )
```

profile of v0, /device:TPU:1, one launch (start us, length us, event | category | flops | bytes accessed | tf_op | source)
XLA Modules:
  0.0 825.5 jit_solution(6142609821865402190)
XLA Ops:
  20.2 4.1 all-gather.1
  41.5 12.0 %multiply_convert_fusion = (bf16[256,3072]{1,0:T(8,128)(2,1)}, f32[256,3072]{1,0:T(8,128)}, f32[256,3072]{1,0:T(8,128)}) fusion(f32[3072]{0:T(1024)} %param.32, bf16[256,768]{1,0:T(8,128)(2,1)S(1)} %fusion.70, bf16[768,3072]{1,0:T(8,128)(2,1)} %param.25), kind=kOutput, calls=%fused_computation.34 | convolution fusion | flops 1259864064 | bytes 12988416 | tf_op jit(solution)/shard_map/dot_general | solution.py:109
  53.5 4.6 fusion.95
  68.6 6.6 add_convert_fusion
  75.2 5.6 multiply_reduce_fusion.1
  95.7 3.6 fusion.96
  99.3 23.1 %multiply_convert_fusion.1 = bf16[12,64,512]{2,1,0:T(8,128)(2,1)} fusion(bf16[256,12,64]{0,2,1:T(8,128)(2,1)} %bitcast.155, bf16[1,12,256,512]{3,2,1,0:T(8,128)(2,1)} %param.37, f32[12,256]{1,0:T(8,128)S(1)} %fusion.4, f32[12,256,512]{2,1,0:T(8,128)} %fusion.96, f32[12,256,512]{2,1,0:T(8,128)} %copy-done.1, f32[12,256]{1,0:T(8,128)} %log_add_fusion, ...), kind=kOutput, calls=%fused_computation.58 | convolution fusion | flops 227282432 | bytes 17064448 | tf_op jit(solution)/shard_map/rhqk,rqhe->rkhe/dot_general | solution.py:163
  135.3 22.7 %fusion.60 = bf16[12,64,256]{2,1,0:T(8,128)(2,1)} fusion(bf16[512,12,64]{0,2,1:T(8,128)(2,1)} %bitcast.152, bf16[1,12,256,512]{3,2,1,0:T(8,128)(2,1)} %param.37, f32[12,256]{1,0:T(8,128)S(1)} %fusion.4, f32[12,256,512]{2,1,0:T(8,128)} %fusion.96, f32[12,256,512]{2,1,0:T(8,128)} %copy-done.1, f32[12,256]{1,0:T(8,128)} %log_add_fusion, ...), kind=kOutput, calls=%fused_computation.67 | convolution fusion | flops 226889216 | bytes 17064448 | tf_op jit(solution)/shard_map/rhqk,rkhe->rqhe/dot_general | solution.py:159
  162.6 4.8 all-reduce.1
  172.9 4.2 all-gather.2
  179.8 4.8 convolution_bitcast_fusion.1
  184.6 5.8 copy.49
  190.5 8.3 %fusion.98 = f32[3072,768]{1,0:T(8,128)} fusion(bf16[512,3072]{1,0:T(8,128)(2,1)} %all-gather.11.cloned.1.call-done, bf16[512,768]{1,0:T(8,128)(2,1)} %copy-done.18), kind=kOutput, calls=%fused_computation.143 | convolution fusion | flops 2415919104 | bytes 13369344 | tf_op jit(solution)/shard_map/nd,ne->de/dot_general | solution.py:24
  198.7 11.0 %reshape.454 = f32[2359296]{0:T(1024)} reshape(f32[3072,768]{1,0:T(8,128)} %fusion.98) | data formatting | bytes 18874368 | tf_op jit(solution)/shard_map/reshape | solution.py:219
  212.3 6.7 convolution_bitcast_fusion
  219.0 8.0 copy.47
  227.0 7.9 reshape.451
  238.9 5.7 constant_dynamic-update-slice_fusion.8
  247.4 9.3 %copy-done.3 = f32[7087104]{0:T(1024)} copy-done((f32[7087104]{0:T(1024)}, f32[7087104]{0:T(1024)S(1)}, u32[]{:S(2)}) %copy-start.3) | copy-done | bytes 28348440
  256.7 129.5 %while.1 = (u32[]{:T(128)}, f32[7087104]{0:T(1024)}, f32[16,2,221472]{2,1,0:T(2,128)}, u32[]{}, u32[]{}, /*index=5*/u32[]{}, u32[]{}) while((u32[]{:T(128)}, f32[7087104]{0:T(1024)}, f32[16,2,221472]{2,1,0:T(2,128)}, u32[]{}, u32[]{}, /*index=5*/u32[]{}, u32[]{}) %tuple.50), condition=%wide.cond, body=%wide.body.sunk | while | flops 9 | bytes 21264564
  256.7 4.8 dynamic-slice.5
  261.5 6.8 reshape.466
  268.3 4.7 constant_dynamic-update-slice_fusion.13
  272.9 4.8 dynamic-slice.5
  277.7 6.8 reshape.466
  284.5 4.7 constant_dynamic-update-slice_fusion.13
  289.1 4.8 dynamic-slice.5
  293.9 6.8 reshape.466
  300.7 4.7 constant_dynamic-update-slice_fusion.13
  305.3 4.8 dynamic-slice.5
  310.1 6.8 reshape.466
  316.8 4.6 constant_dynamic-update-slice_fusion.13
  321.5 4.8 dynamic-slice.5
  326.3 6.8 reshape.466
  333.0 4.7 constant_dynamic-update-slice_fusion.13
  337.7 4.8 dynamic-slice.5
  342.5 6.8 reshape.466
  349.2 4.6 constant_dynamic-update-slice_fusion.13
  353.9 4.8 dynamic-slice.5
  358.6 6.8 reshape.466
  365.4 4.7 constant_dynamic-update-slice_fusion.13
  370.1 4.8 dynamic-slice.5
  374.8 6.8 reshape.466
  381.6 4.6 constant_dynamic-update-slice_fusion.13
  386.2 14.4 %constant_dynamic-slice_fusion = f32[16,1,221472]{2,1,0:T(1,128)S(1)} fusion(f32[16,2,221472]{2,1,0:T(2,128)} %get-tuple-element.7, s32[]{:T(128)S(6)} %select_n.25), kind=kLoop, calls=%fused_computation.125 | loop fusion | bytes 28348420 | tf_op jit(solution)/shard_map/jit(dynamic_index_in_dim)/dynamic_slice | solution.py:233
  400.6 5.7 copy.51
  411.0 394.8 %all-reduce.4.cloned.1.call-done = f32[16,221472]{1,0:T(8,128)} async-done(((f32[16,221472]{1,0:T(8,128)}), f32[16,221472]{1,0:T(8,128)}) %all-reduce.4.cloned.1.call-update) | async-done | bytes 14174224
  805.8 12.4 %dynamic-slice_reduce_fusion = f32[221472]{0:T(1024)} fusion(f32[16,221472]{1,0:T(8,128)} %all-reduce.4.cloned.1.call-done, u32[]{:T(128)} %bitcast.38), kind=kLoop, calls=%fused_computation.75 | loop fusion | bytes 1771780 | tf_op jit(solution)/shard_map/reshape | solution.py:236
  (194 shorter events, 91.9 us)
Async XLA Ops:
  7.2 2.0 copy-start
  7.2 150.9 %reduce-scatter.5.cloned.1.call-start = ((), (), s32[]{:S(2)}) async-start(), calls=%async_computation.3 | async-start | bytes 1179648 | tf_op jit(solution)/shard_map/reduce_scatter | solution.py:175
  26.6 2.4 copy-start.42
  29.0 2.6 copy-start.1
  31.6 1.7 copy-start.25
  31.6 1.8 copy-start.9
  33.3 3.1 copy-start.2
  33.3 2.1 copy-start.12
  33.4 2.5 copy-start.20
  33.4 2.5 copy-start.43
  34.5 3.1 copy-start.15
  36.5 1.7 copy-start.35
  37.6 1.2 copy-start.39
  41.5 12.0 %copy-start.21 = (bf16[256,768]{1,0:T(8,128)(2,1)}, bf16[256,768]{1,0:T(8,128)(2,1)S(1)}, u32[]{:S(2)}) copy-start(bf16[256,768]{1,0:T(8,128)(2,1)S(1)} %fusion.70) | copy-start | bytes 1179652
  60.3 8.3 %copy-start.52 = (f32[256,3072]{1,0:T(8,128)S(1)}, f32[256,3072]{1,0:T(8,128)}, u32[]{:S(2)}) copy-start(f32[256,3072]{1,0:T(8,128)} %get-tuple-element.30) | copy-start | bytes 9437188
  60.9 7.0 copy-start.32
  60.9 6.9 copy-start.28
  60.9 7.0 copy-start.30
  75.1 5.7 copy-start.40
  75.1 5.7 copy-start.5
  75.1 5.7 copy-start.34
  75.1 5.7 copy-start.36
  75.2 5.7 copy-start.38
  80.8 2.1 copy-start.13
  89.7 68.4 %reduce-scatter.3.cloned.1.call-start = ((), (), s32[]{:S(2)}) async-start(), calls=%async_computation.2 | async-start | bytes 1179648 | tf_op jit(solution)/shard_map/reduce_scatter | solution.py:172
  89.8 5.9 copy-start.10
  89.8 5.9 copy-start.14
  122.4 57.4 %all-gather.9.cloned.1.call-start = ((), (), s32[]{:S(2)}) async-start(), calls=%async_computation.5 | async-start | bytes 4718592 | tf_op jit(solution)/shard_map/all_gather | solution.py:206
  123.2 67.3 %all-gather.11.cloned.1.call-start = ((), (), s32[]{:S(2)}) async-start(), calls=%async_computation.6 | async-start | bytes 4718592 | tf_op jit(solution)/shard_map/all_gather | solution.py:207
  123.7 88.5 %all-gather.7.cloned.1.call-start = ((), (), s32[]{:S(2)}) async-start(), calls=%async_computation.4 | async-start | bytes 3538944 | tf_op jit(solution)/shard_map/all_gather | solution.py:202
  158.0 2.7 copy-start.26
  158.0 2.7 copy-start.27
  158.0 2.7 copy-start.29
  158.0 2.7 copy-start.31
  160.6 645.1 %all-reduce.4.cloned.1.call-start = ((), (), s32[]{:S(2)}) async-start(), calls=%async_computation.7 | async-start | bytes 28360704
  167.4 9.7 %copy-start.22 = (bf16[256,768]{1,0:T(8,128)(2,1)S(1)}, bf16[256,768]{1,0:T(8,128)(2,1)}, u32[]{:S(2)}) copy-start(bf16[256,768]{1,0:T(8,128)(2,1)} %copy-done.21) | copy-start | bytes 1179652
  234.9 3.7 copy-start.7
  238.7 5.9 slice-start
  238.8 6.1 slice-start.1
  238.9 6.3 slice-start.2
  245.2 1.7 copy-start.6
  245.2 2.1 copy-start.37
  245.2 2.1 copy-start.47
  245.2 2.1 copy-start.46
  245.2 2.2 copy-start.45
  245.2 2.2 copy-start.44
  247.4 9.3 %copy-start.3 = (f32[7087104]{0:T(1024)}, f32[7087104]{0:T(1024)S(1)}, u32[]{:S(2)}) copy-start(f32[7087104]{0:T(1024)S(1)} %constant_dynamic-update-slice_fusion) | copy-start | bytes 85045248
  406.3 1.3 copy-start.49
  (14 other events, 11.6 us)
Sparse Core Ops, SparseCore 0:
  89.8 10.6 reduce-scatter.4
  122.6 10.7 reduce-scatter.2
  134.9 13.3 all-gather.8
  149.6 13.2 all-gather.10
  164.3 11.8 all-gather.6
  406.5 399.2 all-reduce.3
where the time goes:
time: 836 us; the launch traced here: 825 us
  waiting for transfers between devices  396 us (47%)
  local copies, waits for them, and re-layouts  241 us (29%)
  matrix products  115 us (14%)
  other arithmetic  29.5 us (4%)
  blocking collectives  25.9 us (3%)
  between operations  18 us (2%)
    unnamed x7, waiting for transfers between devices  396 us
    unnamed x151, local copies, waits for them, and re-layouts  175 us
    dot_general x1, matrix products, body(): jnp.einsum('rhqk,rqhe->rkhe', grad_scores, queries, preferred_element_typ...  23.1 us
    dot_general x1, matrix products, body(): jnp.einsum('rhqk,rkhe->rqhe', grad_scores, keys_heads, preferred_element_...  22.7 us
    dot_general x4, matrix products, outer_sum(): jnp.einsum('nd,ne->de', left, right, preferred_element_type=jnp.float32)  22 us
  transfers between devices with their start and end apart: 6, of which 1 were waited for; matrix products, arithmetic and copies ran while one was open for 12% of the time, Pallas kernels for 0%

commit v1 on v0

--- a/solution.py
+++ b/solution.py
@@ -1,13 +1,861 @@
 import jax
 import jax.numpy as jnp
 from jax import lax
+from jax.experimental import pallas as pl
+from jax.experimental.pallas import tpu as pltpu
 from jax.sharding import PartitionSpec as P
 
 HEADS = 12
 HEAD_DIM = 64
-
+WIDTH = 768
+FF = 3072
+BLOCK = 256
+ROW = 512
+UNIT = 288
+CHIPS = 16
+LANES = 128
+
+MESH = pl.DeviceIdType.MESH
+LOW = jnp.bfloat16
+FULL = jnp.float32
 
 norm_eps = 1e-12
+
+
+def dot_nn(left, right):
+    return jnp.dot(left, right, preferred_element_type=FULL)
+
+
+def dot_nt(left, right):
+    return lax.dot_general(left, right, (((1,), (1,)), ((), ())), preferred_element_type=FULL)
+
+
+def dot_tn(left, right):
+    return lax.dot_general(left, right, (((0,), (0,)), ((), ())), preferred_element_type=FULL)
+
+
+def both(own, other):
+    return jnp.concatenate([own, other], axis=0)
+
+
+def col_sum(field):
+    return jnp.sum(field, axis=0, keepdims=True)
+
+
+def row_mean(field):
+    return jnp.mean(field, axis=-1, keepdims=True)
+
+
+def aligned(start, step):
+    return pl.multiple_of(start, step)
+
+
+def layer_kernel(
+    hidden,
+    upstream,
+    teacher,
+    w_project,
+    w_output,
+    w_expand,
+    w_reduce,
+    query_bias,
+    value_bias,
+    output_bias,
+    first_gain,
+    first_shift,
+    expand_bias,
+    reduce_bias,
+    second_gain,
+    second_shift,
+    start_vector,
+    end_vector,
+    valid_length,
+    start_index,
+    end_index,
+    answerable,
+    layer_output,
+    input_gradient,
+    grads,
+    wp,
+    wo,
+    we,
+    wr,
+    te,
+    up,
+    x_row,
+    q_own,
+    k_row,
+    v_row,
+    soft,
+    att_own,
+    att_oth,
+    mix_own,
+    mix_oth,
+    act_own,
+    act_oth,
+    slope,
+    norm_one,
+    resid_two,
+    resid_one,
+    gred_own,
+    gred_oth,
+    gexp_own,
+    gexp_oth,
+    gbr_own,
+    gbr_oth,
+    gatt,
+    qt,
+    gat,
+    dkv_out,
+    dkv_in,
+    gpj_own,
+    gpj_oth,
+    live_map,
+    grad,
+    plane_in,
+    plane_in2,
+    chain_in,
+    total,
+    total_oth,
+    flat,
+    bias_sum,
+    bias_in,
+    load_sem,
+    core_send,
+    core_recv,
+    s1_send,
+    s1_recv,
+    s2_send,
+    s2_recv,
+    chain_send,
+    chain_recv,
+    bias_send,
+    bias_recv,
+    fix_send,
+    fix_recv,
+):
+    dp = lax.axis_index("dp")
+    blk = lax.axis_index("blk")
+    oth = 1 - blk
+    xx = dp % 2
+    yy = (dp // 2) % 2
+    zz = dp // 4
+    core_dev = (dp, oth)
+    x_dev = (dp + 1 - 2 * xx, blk)
+    y_dev = (dp + 2 - 4 * yy, blk)
+    up_dev = (dp + 4, blk)
+    down_dev = (dp - 4, blk)
+    device = dp * 2 + blk
+
+    def load(at, src, dst):
+        copy = pltpu.make_async_copy(src, dst, load_sem.at[at])
+        copy.start()
+        return copy
+
+    own_rows = pl.ds(aligned(blk * BLOCK, BLOCK), BLOCK)
+    oth_rows = pl.ds(aligned(oth * BLOCK, BLOCK), BLOCK)
+    load_x = load(0, hidden, x_row.at[own_rows])
+    load_wp = load(1, w_project, wp)
+    load_wo = load(2, w_output, wo)
+    load_we = load(3, w_expand, we)
+    load_wr = load(4, w_reduce, wr)
+    load_up = load(5, upstream, up)
+    load_te = load(6, teacher, te)
+
+    barrier = pltpu.get_barrier_semaphore()
+
+    def greet(dev):
+        pl.semaphore_signal(barrier, inc=1, device_id=dev, device_id_type=MESH)
+
+    greet(core_dev)
+    greet(x_dev)
+    greet(y_dev)
+
+    @pl.when(zz > 0)
+    def _():
+        greet(down_dev)
+
+    @pl.when(zz < 3)
+    def _():
+        greet(up_dev)
+
+    @pl.when((blk == 1) & (dp < CHIPS - 1))
+    def _():
+        greet((dp + 1, 0))
+
+    def project_cols(rows, at, bias):
+        part = dot_nn(x_row[rows, :], wp[:, pl.ds(at, 256)])
+        if bias is not None:
+            part = part + bias
+        return part.astype(LOW)
+
+    load_x.wait()
+    load_wp.wait()
+    for tile in range(3):
+        cols = slice(256 * tile, 256 * tile + 256)
+        q_part = project_cols(own_rows, 256 * tile, query_bias[:, cols])
+        q_own[:, cols] = q_part * jnp.asarray(HEAD_DIM ** (-0.5), LOW)
+    for tile in range(3):
+        cols = slice(256 * tile, 256 * tile + 256)
+        k_row[own_rows, cols] = project_cols(own_rows, WIDTH + 256 * tile, None)
+        v_row[own_rows, cols] = project_cols(
+            own_rows, 2 * WIDTH + 256 * tile, value_bias[:, cols]
+        )
+
+    waits = 3 + (zz > 0).astype(jnp.int32) + (zz < 3).astype(jnp.int32)
+    waits = waits + ((blk == 0) & (dp > 0)).astype(jnp.int32)
+    pl.semaphore_wait(barrier, waits)
+
+    def to_core(at, src, dst):
+        copy = pltpu.make_async_remote_copy(
+            src_ref=src,
+            dst_ref=dst,
+            send_sem=core_send.at[at],
+            recv_sem=core_recv.at[at],
+            device_id=core_dev,
+            device_id_type=MESH,
+        )
+        copy.start()
+        return copy
+
+    core_copies = []
+    send_x = to_core(0, x_row.at[own_rows], x_row.at[own_rows])
+    core_copies.append(send_x)
+    length = valid_length[0]
+    key_at = lax.broadcasted_iota(jnp.int32, (1, ROW), 1)
+    key_live = key_at < length
+    token_at = blk * BLOCK + lax.broadcasted_iota(jnp.int32, (BLOCK, 1), 0)
+    row_live = (token_at < length).astype(FULL)
+    live_map[...] = jnp.where(key_live, 1.0 / ROW, 0.0) * row_live
+    pltpu.make_async_remote_copy(
+        src_ref=x_row.at[oth_rows],
+        dst_ref=x_row.at[oth_rows],
+        send_sem=core_send.at[0],
+        recv_sem=core_recv.at[0],
+        device_id=core_dev,
+        device_id_type=MESH,
+    ).wait_recv()
+    for tile in range(3):
+        cols = slice(256 * tile, 256 * tile + 256)
+        k_row[oth_rows, cols] = project_cols(oth_rows, WIDTH + 256 * tile, None)
+        v_row[oth_rows, cols] = project_cols(
+            oth_rows, 2 * WIDTH + 256 * tile, value_bias[:, cols]
+        )
+
+    lane = lax.broadcasted_iota(jnp.int32, (1, LANES), 1)
+    head_lanes = ((lane < HEAD_DIM).astype(LOW), (lane >= HEAD_DIM).astype(LOW))
+
+    @pl.loop(0, HEADS // 2)
+    def _(pair):
+        cols = pl.ds(aligned(pair * LANES, LANES), LANES)
+        q_pair = q_own[:, cols]
+        k_pair = k_row[:, cols]
+        v_pair = v_row[:, cols]
+        gathered = None
+        for side in range(2):
+            scores = dot_nt(q_pair * head_lanes[side], k_pair)
+            scores = jnp.where(key_live, scores, -1e30)
+            peak = jnp.max(scores, axis=-1, keepdims=True)
+            terms = jnp.exp(scores - peak)
+            scale = 1.0 / jnp.sum(terms, axis=-1, keepdims=True)
+            soft_low = (terms * scale).astype(LOW)
+            soft[2 * pair + side] = soft_low
+            part = dot_nn(soft_low, v_pair * head_lanes[side])
+            gathered = part if gathered is None else gathered + part
+        att_own[:, cols] = gathered.astype(LOW)
+
+    core_copies.append(to_core(1, att_own, att_oth))
+
+    load_wo.wait()
+    branch = dot_nn(att_own[...], wo[...]) + output_bias[...]
+    resid = x_row[own_rows, :].astype(FULL) + branch
+    centre = resid - row_mean(resid)
+    scale_one = lax.rsqrt(row_mean(centre * centre) + norm_eps)
+    normal = centre * scale_one
+    norm_one[...] = normal
+    mix_own[...] = (normal * first_gain[...] + first_shift[...]).astype(LOW)
+    core_copies.append(to_core(2, mix_own, mix_oth))
+
+    load_we.wait()
+
+    @pl.loop(0, 6)
+    def _(at):
+        cols = pl.ds(aligned(at * 512, 512), 512)
+        expanded = dot_nn(mix_own[...], we[:, cols]) + expand_bias[:, cols]
+        gate = 0.5 + 0.5 * lax.erf(expanded * (2.0**-0.5))
+        bell = jnp.exp(expanded * expanded * -0.5) * ((2.0 * jnp.pi) ** -0.5)
+        act_own[:, cols] = (expanded * gate).astype(LOW)
+        slope[:, cols] = (gate + expanded * bell).astype(LOW)
+
+    core_copies.append(to_core(3, act_own, act_oth))
+    load_wr.wait()
+    reduced = dot_nn(act_own[...], wr[...]) + reduce_bias[...]
+    mixed = norm_one[...] * first_gain[...] + first_shift[...]
+    resid = mixed + reduced
+    centre = resid - row_mean(resid)
+    scale_two = lax.rsqrt(row_mean(centre * centre) + norm_eps)
+    normal = centre * scale_two
+    layer_output[...] = (normal * second_gain[...] + second_shift[...]).astype(LOW)
+
+    answered = answerable[0] > 0
+    start_slot = jnp.where(answered, start_index[0], 0)
+    end_slot = jnp.where(answered, end_index[0], 0)
+    load_up.wait()
+    cot = up[...].astype(FULL) * row_live
+    cot = cot + (token_at == start_slot).astype(FULL) * start_vector[...]
+    cot = cot + (token_at == end_slot).astype(FULL) * end_vector[...]
+
+    def put_bias(first_row, vector):
+        for at in range(vector.shape[1] // LANES):
+            bias_sum[first_row + at : first_row + at + 1, :] = vector[
+                :, at * LANES : (at + 1) * LANES
+            ]
+
+    put_bias(60, col_sum(cot * normal))
+    put_bias(66, col_sum(cot))
+    pulled = cot * second_gain[...]
+    pulled = scale_two * (pulled - row_mean(pulled) - normal * row_mean(pulled * normal))
+    resid_two[...] = pulled
+    pulled_low = pulled.astype(LOW)
+    gred_own[...] = pulled_low
+    put_bias(54, col_sum(pulled_low.astype(FULL)))
+    own_384 = pl.ds(aligned(blk * 384, 384), 384)
+    oth_384 = pl.ds(aligned(oth * 384, 384), 384)
+    core_copies.append(to_core(4, gred_own.at[:, oth_384], gred_oth))
+
+    def send(src, dst, send_sem, recv_sem, dev):
+        pltpu.make_async_remote_copy(
+            src_ref=src,
+            dst_ref=dst,
+            send_sem=send_sem,
+            recv_sem=recv_sem,
+            device_id=dev,
+            device_id_type=MESH,
+        ).start()
+
+    def wait_recv(dst, recv_sem):
+        pltpu.make_async_remote_copy(
+            src_ref=dst,
+            dst_ref=dst,
+            send_sem=recv_sem,
+            recv_sem=recv_sem,
+            device_id=core_dev,
+            device_id_type=MESH,
+        ).wait_recv()
+
+    def wait_send(src, send_sem):
+        pltpu.make_async_remote_copy(
+            src_ref=src,
+            dst_ref=src,
+            send_sem=send_sem,
+            recv_sem=send_sem,
+            device_id=core_dev,
+            device_id_type=MESH,
+        ).wait_send()
+
+    def base_of(plane, x_at, y_at):
+        return 24 * plane + 6 * (2 * y_at + x_at)
+
+    def first_sends(plane):
+        return (
+            (base_of(plane, 1 - xx, 1 - yy), 0, x_dev),
+            (base_of(plane, 1 - xx, 1 - yy) + 3, 2, y_dev),
+            (base_of(plane, 1 - xx, yy), 1, x_dev),
+            (base_of(plane, xx, 1 - yy) + 3, 3, y_dev),
+        )
+
+    def step_one(plane):
+        for first, slot, dev in first_sends(plane):
+            send(
+                grad.at[pl.ds(first, 3)],
+                plane_in.at[plane, slot],
+                s1_send.at[plane, slot],
+                s1_recv.at[plane, slot],
+                dev,
+            )
+
+    def second_sends(plane):
+        return (
+            (base_of(plane, xx, 1 - yy), 0, 0, y_dev),
+            (base_of(plane, 1 - xx, yy) + 3, 2, 1, x_dev),
+        )
+
+    def add_units(first, arrays):
+        @pl.loop(0, 3)
+        def _(at):
+            value = grad[first + at].astype(FULL)
+            for array, index in arrays:
+                value = value + array[index + (at,)].astype(FULL)
+            grad[first + at] = value.astype(LOW)
+
+    def step_two(plane):
+        for first, slot, slot2, dev in second_sends(plane):
+            wait_recv(plane_in.at[plane, slot], s1_recv.at[plane, slot])
+            add_units(first, [(plane_in, (plane, slot))])
+            send(
+                grad.at[pl.ds(first, 3)],
+                plane_in2.at[plane, slot2],
+                s2_send.at[plane, slot2],
+                s2_recv.at[plane, slot2],
+                dev,
+            )
+
+    def step_three(plane):
+        own = base_of(plane, xx, yy)
+        for slot, slot2, first in ((1, 0, own), (3, 1, own + 3)):
+            wait_recv(plane_in.at[plane, slot], s1_recv.at[plane, slot])
+            wait_recv(plane_in2.at[plane, slot2], s2_recv.at[plane, slot2])
+            add_units(first, [(plane_in, (plane, slot)), (plane_in2, (plane, slot2))])
+
+    def chain(plane):
+        own = base_of(plane, xx, yy)
+        below = zz < plane
+        way = jnp.where(below, 0, 1)
+
+        @pl.when(zz != plane)
+        def _():
+            for half in range(2):
+                first = own + 3 * half
+
+                @pl.when((below & (zz > 0)) | (jnp.logical_not(below) & (zz < 3)))
+                def _():
+                    wait_recv(chain_in.at[way, plane, half], chain_recv.at[way, plane, half])
+                    add_units(first, [(chain_in, (way, plane, half))])
+
+                send(
+                    grad.at[pl.ds(first, 3)],
+                    chain_in.at[way, plane, half],
+                    chain_send.at[plane, half],
+                    chain_recv.at[way, plane, half],
+                    (jnp.where(below, dp + 4, dp - 4), blk),
+                )
+
+        @pl.when(zz == plane)
+        def _():
+            for half in range(2):
+                ways = ([0] if plane > 0 else []) + ([1] if plane < 3 else [])
+                for one in ways:
+                    wait_recv(chain_in.at[one, plane, half], chain_recv.at[one, plane, half])
+
+                @pl.loop(0, 3)
+                def _(at):
+                    value = grad[own + 3 * half + at].astype(FULL)
+                    for one in ways:
+                        value = value + chain_in[one, plane, half, at].astype(FULL)
+                    total[3 * half + at] = value
+
+    core_copies[3].wait_recv()
+    core_copies[4].wait_recv()
+
+    def reduce_rows(at):
+        cols = pl.ds(aligned(at * WIDTH, WIDTH), WIDTH)
+        part = dot_tn(
+            both(act_own[:, cols], act_oth[:, cols]), both(gred_own[:, own_384], gred_oth[...])
+        )
+        for unit in range(8):
+            for tile in range(3):
+                grad[64 + 8 * at + unit, 96 * tile : 96 * tile + 96, :] = part[
+                    96 * unit : 96 * unit + 96, LANES * tile : LANES * tile + LANES
+                ].astype(LOW)
+
+    @pl.loop(1, 4)
+    def _(at):
+        reduce_rows(at)
+
+    step_one(3)
+    reduce_rows(0)
+
+    @pl.loop(0, 6)
+    def _(at):
+        half = jnp.where(at < 3, oth, blk)
+        part_at = lax.rem(at, 3) * 512
+        cols = pl.ds(aligned(half * 1536 + part_at, 512), 512)
+        grad_active = dot_nt(gred_own[...], wr[cols, :])
+        grad_expanded = (grad_active * slope[:, cols].astype(FULL)).astype(LOW)
+        gexp_own[half, :, pl.ds(aligned(part_at, 512), 512)] = grad_expanded
+        sums = col_sum(grad_expanded.astype(FULL))
+        for tile in range(4):
+            bias_sum[pl.ds(30 + half * 12 + lax.rem(at, 3) * 4 + tile, 1), :] = sums[
+                :, LANES * tile : LANES * tile + LANES
+            ]
+
+    core_copies.append(to_core(5, gexp_own.at[oth], gexp_oth))
+    grad_mixed = resid_two[...]
+    for half in range(2):
+        grad_mixed = grad_mixed + dot_nt(
+            gexp_own[half], we[:, 1536 * half : 1536 * half + 1536]
+        )
+
+    normal = norm_one[...]
+    put_bias(18, col_sum(grad_mixed * normal))
+    put_bias(24, col_sum(grad_mixed))
+    pulled = grad_mixed * first_gain[...]
+    pulled = scale_one * (pulled - row_mean(pulled) - normal * row_mean(pulled * normal))
+    resid_one[...] = pulled
+    pulled_low = pulled.astype(LOW)
+    gbr_own[...] = pulled_low
+    put_bias(12, col_sum(pulled_low.astype(FULL)))
+    core_copies.append(to_core(6, gbr_own.at[:, oth_384], gbr_oth))
+
+    core_copies[2].wait_recv()
+    core_copies[5].wait_recv()
+
+    @pl.loop(0, 6)
+    def _(at):
+        cols = pl.ds(aligned(at * 256, 256), 256)
+        part = dot_tn(
+            both(mix_own[...], mix_oth[...]), both(gexp_own[blk, :, cols], gexp_oth[:, cols])
+        )
+        rows = pl.ds(aligned(at * 48, 48), 48)
+        for unit in range(32):
+            piece = part[24 * unit : 24 * unit + 24, :]
+            grad[32 + unit, rows, :] = both(piece[:, :LANES], piece[:, LANES:]).astype(LOW)
+
+    step_one(2)
+
+    gatt[...] = dot_nt(gbr_own[...], wo[...]).astype(LOW)
+    core_copies[1].wait_recv()
+    core_copies[6].wait_recv()
+    part = dot_tn(both(att_own[...], att_oth[...]), both(gbr_own[:, own_384], gbr_oth[...]))
+    for unit in range(8):
+        for tile in range(3):
+            grad[24 + unit, 96 * tile : 96 * tile + 96, :] = part[
+                96 * unit : 96 * unit + 96, LANES * tile : LANES * tile + LANES
+            ].astype(LOW)
+    step_one(1)
+
+    qt[...] = q_own[...].T
+    gat[...] = gatt[...].T
+    load_te.wait()
+
+    def head_pair(pair):
+        cols = pl.ds(aligned(pair * LANES, LANES), LANES)
+        ga_pair = gatt[:, cols]
+        k_pair = k_row[:, cols]
+        v_pair = v_row[:, cols]
+        grad_query = None
+        for side in range(2):
+            rows = pl.ds(aligned(pair * LANES + side * HEAD_DIM, HEAD_DIM), HEAD_DIM)
+            soft_low = soft[2 * pair + side]
+            grad_soft = dot_nt(ga_pair * head_lanes[side], v_pair)
+            soft_full = soft_low.astype(FULL)
+            taught = te[2 * pair + side].astype(FULL) * live_map[...]
+            shift = jnp.sum(taught - grad_soft * soft_full, axis=-1, keepdims=True)
+            grad_scores = (soft_full * (grad_soft + shift) - taught).astype(LOW)
+            part = dot_nn(grad_scores, k_pair * head_lanes[side])
+            grad_query = part if grad_query is None else grad_query + part
+            slot = pl.ds(aligned(pair * ROW, ROW), ROW)
+            at = side * HEAD_DIM
+            slope[at : at + HEAD_DIM, slot] = dot_nn(qt[rows, :], grad_scores).astype(LOW)
+            at = at + LANES
+            slope[at : at + HEAD_DIM, slot] = dot_nn(gat[rows, :], soft_low).astype(LOW)
+        gpj_own[:, cols] = (grad_query * HEAD_DIM ** (-0.5)).astype(LOW)
+
+    @pl.loop(0, HEADS // 2)
+    def _(pair):
+        head_pair(pair)
+
+    def turned(pair, block, first):
+        lanes = pl.ds(aligned(pair * ROW + block * BLOCK, BLOCK), BLOCK)
+        return slope[first : first + LANES, lanes].T
+
+    for pair in range(HEADS // 2):
+        for first in (0, LANES):
+            at = pair * LANES + first * (WIDTH // LANES)
+            dkv_out[:, at : at + LANES] = turned(pair, oth, first)
+    core_copies.append(to_core(7, dkv_out, dkv_in))
+    step_two(3)
+    core_copies[7].wait_recv()
+    for pair in range(HEADS // 2):
+        for first in (0, LANES):
+            at = pair * LANES + first * (WIDTH // LANES)
+            gpj_own[:, WIDTH + at : WIDTH + at + LANES] = (
+                turned(pair, blk, first).astype(FULL) + dkv_in[:, at : at + LANES].astype(FULL)
+            ).astype(LOW)
+    own_1152 = pl.ds(aligned(blk * 1152, 1152), 1152)
+    oth_1152 = pl.ds(aligned(oth * 1152, 1152), 1152)
+    core_copies.append(to_core(8, gpj_own.at[:, oth_1152], gpj_oth))
+    put_bias(0, col_sum(gpj_own[:, :WIDTH].astype(FULL)))
+    put_bias(6, col_sum(gpj_own[:, 2 * WIDTH :].astype(FULL)))
+    input_gradient[...] = (resid_one[...] + dot_nt(gpj_own[...], wp[...])).astype(LOW)
+
+    core_copies[8].wait_recv()
+
+    @pl.loop(0, 3)
+    def _(at):
+        cols = pl.ds(aligned(at * 384, 384), 384)
+        mine = pl.ds(aligned(blk * 1152 + at * 384, 384), 384)
+        part = dot_tn(
+            both(x_row[own_rows, :], x_row[oth_rows, :]), both(gpj_own[:, mine], gpj_oth[:, cols])
+        )
+        for unit in range(24):
+            for tile in range(3):
+                rows = pl.ds(aligned(at * 96 + 32 * tile, 32), 32)
+                grad[unit, rows, :] = part[
+                    32 * unit : 32 * unit + 32, LANES * tile : LANES * tile + LANES
+                ].astype(LOW)
+
+    step_one(0)
+
+    def bias_hop(at, here, there, dev):
+        @pl.when(here)
+        def _():
+            send(bias_sum, bias_in.at[at], bias_send.at[0], bias_recv.at[at], dev)
+
+        @pl.when(there)
+        def _():
+            wait_recv(bias_in.at[at], bias_recv.at[at])
+            bias_sum[...] += bias_in[at]
+
+    bias_hop(0, xx == 0, xx == 1, x_dev)
+    step_two(2)
+    step_three(3)
+    chain(3)
+    bias_hop(1, (xx == 1) & (yy == 0), (xx == 1) & (yy == 1), y_dev)
+    step_two(1)
+    step_three(2)
+    chain(2)
+    corner = (xx == 1) & (yy == 1)
+
+    @pl.when(corner & (zz > 0))
+    def _():
+        wait_recv(bias_in.at[2], bias_recv.at[2])
+        bias_sum[...] += bias_in[2]
+
+    @pl.when(corner & (zz < 3))
+    def _():
+        send(bias_sum, bias_in.at[2], bias_send.at[0], bias_recv.at[2], up_dev)
+
+    step_two(0)
+    step_three(1)
+    chain(1)
+    last = dp == CHIPS - 1
+
+    @pl.when(last & (blk == 0))
+    def _():
+        send(bias_sum, bias_in.at[3], bias_send.at[0], bias_recv.at[3], core_dev)
+
+    @pl.when(last & (blk == 1))
+    def _():
+        wait_recv(bias_in.at[3], bias_recv.at[3])
+        flat[1728:1800, :] = bias_sum[...] + bias_in[3]
+
+    step_three(0)
+    chain(0)
+
+    last_send = to_core(9, total.at[pl.ds(3 * oth, 3)], total_oth)
+    core_copies.append(last_send)
+
+    def lay_out(source, first, column_half):
+        for unit in range(3):
+            kind_at = 3 * device + unit
+            kinds = (
+                (kind_at < 24, 32, 9),
+                (((kind_at >= 24) & (kind_at < 32)) | (kind_at >= 64), 96, 3),
+                ((kind_at >= 32) & (kind_at < 64), 24, 12),
+            )
+            for fits, rows, tiles in kinds:
+
+                @pl.when(fits)
+                def _():
+                    for tile in range(tiles):
+                        for group in range(rows // 8):
+                            at = rows * tile + 8 * group
+                            to = 576 * unit + 16 * group * tiles + tile + column_half * tiles
+                            flat[pl.ds(to, 8, stride=2 * tiles), :] = source[
+                                first + unit, at : at + 8, :
+                            ]
+
+    lay_out(total, 3 * blk, blk)
+    last_send.wait_recv()
+    lay_out(total_oth, 0, oth)
+
+    @pl.when(blk == 1)
+    def _():
+        send(flat.at[0:72], flat.at[1728:1800], fix_send.at[0], fix_recv.at[0], core_dev)
+
+    @pl.when((blk == 0) & (dp > 0))
+    def _():
+        send(flat.at[0:72], flat.at[1728:1800], fix_send.at[0], fix_recv.at[0], (dp - 1, 1))
+
+    @pl.when(device < 2 * CHIPS - 1)
+    def _():
+        wait_recv(flat.at[1728:1800], fix_recv.at[0])
+
+    shift = 32 * lax.rem(device, 4)
+    skip = (9 * device) // 4
+    stays = lane < LANES - shift
+
+    @pl.loop(0, 31)
+    def _(at):
+        rows = at * 56
+        first = pltpu.roll(flat[pl.ds(rows + skip, 56), :], LANES - shift, 1)
+        second = pltpu.roll(flat[pl.ds(rows + skip + 1, 56), :], LANES - shift, 1)
+        grads[pl.ds(aligned(rows, 8), 56), :] = jnp.where(stays, first, second)
+
+    for copy in core_copies:
+        copy.wait_send()
+    for plane in range(4):
+        for slot in range(4):
+            wait_send(plane_in.at[plane, slot], s1_send.at[plane, slot])
+        for slot in range(2):
+            wait_send(plane_in2.at[plane, slot], s2_send.at[plane, slot])
+
+        @pl.when(zz != plane)
+        def _():
+            for half in range(2):
+                wait_send(chain_in.at[0, plane, half], chain_send.at[plane, half])
+
+    @pl.when(jnp.logical_not(last & (blk == 1)))
+    def _():
+        wait_send(bias_sum, bias_send.at[0])
+
+    @pl.when(device > 0)
+    def _():
+        wait_send(flat.at[0:72], fix_send.at[0])
+
+
+def fused_layer(
+    hidden_in,
+    project_weight,
+    output_weight,
+    expand_weight,
+    reduce_weight,
+    query_bias,
+    value_bias,
+    output_bias,
+    first_gain,
+    first_shift,
+    expand_bias,
+    reduce_bias,
+    second_gain,
+    second_shift,
+    upstream,
+    teacher_maps,
+    start_vector,
+    end_vector,
+    valid_length,
+    start_index,
+    end_index,
+    answerable,
+):
+    vectors = [
+        vector.reshape(1, -1)
+        for vector in (
+            query_bias,
+            value_bias,
+            output_bias,
+            first_gain,
+            first_shift,
+            expand_bias,
+            reduce_bias,
+            second_gain,
+            second_shift,
+            start_vector,
+            end_vector,
+        )
+    ]
+    scalars = [valid_length, start_index, end_index, answerable]
+    anywhere = pl.BlockSpec(memory_space=pl.ANY)
+    in_vmem = pl.BlockSpec(memory_space=pltpu.VMEM)
+    in_smem = pl.BlockSpec(memory_space=pltpu.SMEM)
+
+    def low(*shape):
+        return pltpu.VMEM(shape, LOW)
+
+    def full(*shape):
+        return pltpu.VMEM(shape, FULL)
+
+    dma = pltpu.SemaphoreType.DMA
+    scratch = [
+        low(WIDTH, 3 * WIDTH),
+        low(WIDTH, WIDTH),
+        low(WIDTH, FF),
+        low(FF, WIDTH),
+        low(HEADS, BLOCK, ROW),
+        low(BLOCK, WIDTH),
+        low(ROW, WIDTH),
+        low(BLOCK, WIDTH),
+        low(ROW, WIDTH),
+        low(ROW, WIDTH),
+        low(HEADS, BLOCK, ROW),
+        low(BLOCK, WIDTH),
+        low(BLOCK, WIDTH),
+        low(BLOCK, WIDTH),
+        low(BLOCK, WIDTH),
+        low(BLOCK, FF),
+        low(BLOCK, FF),
+        low(BLOCK, FF),
+        full(BLOCK, WIDTH),
+        full(BLOCK, WIDTH),
+        full(BLOCK, WIDTH),
+        low(BLOCK, WIDTH),
+        low(BLOCK, WIDTH // 2),
+        low(2, BLOCK, FF // 2),
+        low(BLOCK, FF // 2),
+        low(BLOCK, WIDTH),
+        low(BLOCK, WIDTH // 2),
+        low(BLOCK, WIDTH),
+        low(WIDTH, BLOCK),
+        low(WIDTH, BLOCK),
+        low(BLOCK, 2 * WIDTH),
+        low(BLOCK, 2 * WIDTH),
+        low(BLOCK, 3 * WIDTH),
+        low(BLOCK, 3 * WIDTH // 2),
+        full(BLOCK, ROW),
+        low(96, UNIT, LANES),
+        low(4, 4, 3, UNIT, LANES),
+        low(4, 2, 3, UNIT, LANES),
+        low(2, 4, 2, 3, UNIT, LANES),
+        full(6, UNIT, LANES),
+        full(3, UNIT, LANES),
+        full(1816, LANES),
+        full(72, LANES),
+        full(4, 72, LANES),
+        dma((7,)),
+        dma((10,)),
+        dma((10,)),
+        dma((4, 4)),
+        dma((4, 4)),
+        dma((4, 2)),
+        dma((4, 2)),
+        dma((4, 2)),
+        dma((2, 4, 2)),
+        dma((1,)),
+        dma((4,)),
+        dma((1,)),
+        dma((1,)),
+    ]
+    layer_output, input_gradient, grads = pl.pallas_call(
+        layer_kernel,
+        out_shape=(
+            jax.ShapeDtypeStruct((BLOCK, WIDTH), LOW),
+            jax.ShapeDtypeStruct((BLOCK, WIDTH), LOW),
+            jax.ShapeDtypeStruct((1736, LANES), FULL),
+        ),
+        in_specs=[anywhere] * 7 + [in_vmem] * len(vectors) + [in_smem] * 4,
+        out_specs=(in_vmem, in_vmem, in_vmem),
+        scratch_shapes=scratch,
+        compiler_params=pltpu.CompilerParams(
+            collective_id=0, has_side_effects=True, vmem_limit_bytes=63 * 2**20
+        ),
+        name="encoder_layer",
+    )(
+        hidden_in.reshape(BLOCK, WIDTH),
+        upstream.reshape(BLOCK, WIDTH),
+        teacher_maps.reshape(HEADS, BLOCK, ROW),
+        project_weight,
+        output_weight,
+        expand_weight,
+        reduce_weight,
+        *vectors,
+        *scalars,
+    )
+    return (
+        layer_output.reshape(1, BLOCK, WIDTH),
+        input_gradient.reshape(1, BLOCK, WIDTH),
+        grads.reshape(-1)[: 96 * 3 * 576 * LANES // 96 + 288],
+    )
 
 
 def layer_norm(field_in, gain_vec, shift_vec):
@@ -28,7 +876,7 @@
     return jnp.sum(values_low.astype(jnp.float32), axis=0)
 
 
-def body(
+def plain_layer(
     hidden_in,
     project_weight,
     output_weight,
@@ -264,8 +1112,10 @@
         P("dp"),
         P("dp"),
     )
+    fits = (mesh.shape["dp"], mesh.shape["blk"]) == (CHIPS, 2)
+    layer = fused_layer if fits else plain_layer
     return jax.shard_map(
-        body,
+        layer,
         mesh=mesh,
         in_specs=placed,
         out_specs=(P("dp", "blk", None), P("dp", "blk", None), P(("dp", "blk"))),

time: 836 us -> 161 us (0.19)
  waiting for transfers between devices: 396 us -> 0 us
  local copies, waits for them, and re-layouts: 241 us -> 18.4 us
  Pallas kernels: 0 us -> 137 us
  matrix products: 115 us -> 0 us
  other arithmetic: 29.5 us -> 0 us
  blocking collectives: 25.9 us -> 0 us
  between operations: 18 us -> 3.23 us
    unnamed x7 -> x0, waiting for transfers between devices: 396 us -> none
    unnamed x151 -> x3, local copies, waits for them, and re-layouts: 175 us -> 5.67 us
    pallas_call x0 -> x1, Pallas kernels: none -> 137 us  [fused_layer(): pl.pallas_call(layer_kernel, out_shape=(jax.ShapeDtypeStruct((BLOCK, WIDT...]
    dot_general x18 -> x0, matrix products: 115 us -> none  [the longest x1 23.1 us: body(): jnp.einsum('rhqk,rqhe->rkhe', grad_scores, queries, preferred_element_typ...]
    reshape x4 -> x10, local copies, waits for them, and re-layouts: 34.6 us -> 12.7 us  [fused_layer(): vector.reshape(1, -1)]
    all_gather x7 -> x0, blocking collectives: 21.1 us -> none  [the longest x1 4.19 us: body(): lax.all_gather(tokens, 'blk', axis=0, tiled=True)]
    reduce_sum x12 -> x0, other arithmetic: 17.6 us -> none  [the longest x4 4.98 us: column_sum(): return jnp.sum(values_low.astype(jnp.float32), axis=0)]
    dynamic_slice x1 -> x0, local copies, waits for them, and re-layouts: 14.4 us -> none  [body(): lax.dynamic_index_in_dim(flat_grads.reshape(data_count, blocks, piece_len...]
  transfers between devices with their start and end apart: 6 -> 0, of which waited for: 1 -> 0; matrix products, arithmetic and copies ran while one was open for 12% -> 0% of each run, Pallas kernels for 0% -> 0%
where the time goes in v1:
time: 161 us; the launch traced here: 159 us
  Pallas kernels  137 us (85%)
  local copies, waits for them, and re-layouts  18.4 us (11%)
  between operations  3.23 us (2%)
    pallas_call x1, Pallas kernels, fused_layer(): pl.pallas_call(layer_kernel, out_shape=(jax.ShapeDtypeStruct((BLOCK, WIDT...  137 us
    reshape x10, local copies, waits for them, and re-layouts, fused_layer(): vector.reshape(1, -1)  12.7 us
    unnamed x3, local copies, waits for them, and re-layouts  5.67 us

profile of v1, /device:TPU:1, one launch (start us, length us, event | category | flops | bytes accessed | tf_op | source)
XLA Modules:
  0.0 158.5 jit_solution(1752343968431152367)
XLA Ops:
  3.2 1.3 reshape.60.query_bias
  4.5 1.3 reshape.61.value_bias
  5.7 1.3 reshape.62.output_bias
  7.0 1.3 reshape.63.first_gain
  8.3 1.3 reshape.64.first_shift
  9.6 1.3 reshape.66.reduce_bias
  10.8 1.3 reshape.67.second_gain
  12.1 1.3 reshape.68.second_shift
  13.4 1.3 reshape.69.start_vector
  14.7 1.3 reshape.70.end_vector
  15.9 136.9 %encoder_layer.1 = (bf16[256,768]{1,0:T(8,128)(2,1)}, bf16[256,768]{1,0:T(8,128)(2,1)}, f32[1736,128]{1,0:T(8,128)}) custom-call(bf16[256,768]{1,0:T(8,128)(2,1)} %bitcast.12, bf16[256,768]{1,0:T(8,128)(2,1)} %bitcast.13, bf16[12,256,512]{2,1,0:T(8,128)(2,1)} %bitcast.8, bf16[768,2304]{1,0:T(8,128)(2,1)} %w_project.1, bf16[768,768]{1,0:T(8,128)(2,1)} %w_output.1, ...), custom_call_target="tpu_custom_call" | custom-call | tf_op jit(solution)/shard_map/encoder_layer/pallas_call | solution.py:829
  152.9 1.8 %copy.32 = bf16[1,256,768]{2,1,0:T(8,128)(2,1)} copy(bf16[1,256,768]{2,1,0:T(8,128)(2,1)} %bitcast.11) | data formatting | bytes 786432
  154.6 1.8 %copy.33 = bf16[1,256,768]{2,1,0:T(8,128)(2,1)} copy(bf16[1,256,768]{2,1,0:T(8,128)(2,1)} %bitcast.10) | data formatting | bytes 786432
  156.4 2.1 %copy.34 = f32[221472]{0:T(1024)} copy(f32[221472]{0:T(1024)} %bitcast.9) | data formatting | bytes 1771776

commit v2 on v1

--- a/solution.py
+++ b/solution.py
@@ -46,6 +46,81 @@
     return jnp.mean(field, axis=-1, keepdims=True)
 
 
+SCHEDULE = {
+    "reduce": (
+        ("first", 3, 1),
+    ),
+    "slopes": (
+        ("first", 3, 0),
+    ),
+    "norm": (
+        ("second", 3, 1),
+    ),
+    "expand": (
+        ("pair", 2, 2),
+        ("pair", 3, 2),
+        ("second", 3, 0),
+    ),
+    "output": (
+        ("first", 1, 1),
+    ),
+    "heads0": (
+        ("first", 1, 0),
+    ),
+    "heads2": (
+        ("second", 1, 1),
+        ("first", 2, 0),
+    ),
+    "keys": (
+        ("pair", 1, 2),
+    ),
+    "project": (
+        ("first", 0, 0),
+        ("pair", 0, 2),
+        ("add", 3, 2),
+        ("second", 3, 2),
+        ("second", 2, 0),
+        ("third", 3, 1),
+    ),
+    "bias0": (
+        ("second", 0, 0),
+        ("first", 0, 1),
+        ("third", 3, 0),
+        ("second", 1, 0),
+        ("third", 1, 1),
+        ("add", 2, 2),
+    ),
+    "bias1": (
+        ("third", 0, 0),
+        ("second", 0, 1),
+        ("third", 2, 0),
+        ("add", 0, 2),
+        ("first", 2, 1),
+        ("third", 3, 2),
+    ),
+    "bias2": (
+        ("third", 1, 0),
+        ("third", 0, 1),
+        ("second", 0, 2),
+        ("second", 2, 1),
+        ("add", 1, 2),
+        ("second", 1, 2),
+    ),
+    "bias3": (
+        ("third", 0, 2),
+        ("third", 2, 1),
+        ("second", 2, 2),
+        ("third", 2, 2),
+        ("third", 1, 2),
+        ("finish", 0, 0),
+        ("finish", 0, 1),
+    ),
+    "end1": (
+        ("finish", 0, 2),
+    ),
+}
+
+
 def aligned(start, step):
     return pl.multiple_of(start, step)
 
@@ -58,21 +133,8 @@
     w_output,
     w_expand,
     w_reduce,
-    query_bias,
-    value_bias,
-    output_bias,
-    first_gain,
-    first_shift,
-    expand_bias,
-    reduce_bias,
-    second_gain,
-    second_shift,
-    start_vector,
-    end_vector,
-    valid_length,
-    start_index,
-    end_index,
-    answerable,
+    vectors,
+    scalars,
     layer_output,
     input_gradient,
     grads,
@@ -83,6 +145,7 @@
     te,
     up,
     x_row,
+    vector_at,
     q_own,
     k_row,
     v_row,
@@ -111,28 +174,36 @@
     gpj_own,
     gpj_oth,
     live_map,
+    out_own,
+    gin_own,
     grad,
-    plane_in,
-    plane_in2,
-    chain_in,
+    pair_in,
+    first_in,
+    second_in,
+    far_in,
     total,
     total_oth,
     flat,
+    placed,
     bias_sum,
     bias_in,
     load_sem,
+    vector_sem,
     core_send,
     core_recv,
-    s1_send,
-    s1_recv,
-    s2_send,
-    s2_recv,
-    chain_send,
-    chain_recv,
+    pair_send,
+    pair_recv,
+    first_send,
+    first_recv,
+    second_send,
+    second_recv,
+    far_send,
+    far_recv,
     bias_send,
     bias_recv,
     fix_send,
     fix_recv,
+    out_sem,
 ):
     dp = lax.axis_index("dp")
     blk = lax.axis_index("blk")
@@ -140,11 +211,12 @@
     xx = dp % 2
     yy = (dp // 2) % 2
     zz = dp // 4
+    column = dp % 4
+    outer = (zz == 0) | (zz == 3)
     core_dev = (dp, oth)
     x_dev = (dp + 1 - 2 * xx, blk)
     y_dev = (dp + 2 - 4 * yy, blk)
-    up_dev = (dp + 4, blk)
-    down_dev = (dp - 4, blk)
+    pair_dev = (jnp.where(zz % 2 == 0, dp + 4, dp - 4), blk)
     device = dp * 2 + blk
 
     def load(at, src, dst):
@@ -156,11 +228,29 @@
     oth_rows = pl.ds(aligned(oth * BLOCK, BLOCK), BLOCK)
     load_x = load(0, hidden, x_row.at[own_rows])
     load_wp = load(1, w_project, wp)
+    small = []
+    for at, (src, dst) in enumerate(zip(vectors, vector_at)):
+        small.append(pltpu.make_async_copy(src, dst.at[0], vector_sem.at[at]))
+    for copy in small:
+        copy.start()
     load_wo = load(2, w_output, wo)
     load_we = load(3, w_expand, we)
     load_wr = load(4, w_reduce, wr)
     load_up = load(5, upstream, up)
     load_te = load(6, teacher, te)
+    (
+        query_bias,
+        value_bias,
+        output_bias,
+        first_gain,
+        first_shift,
+        expand_bias,
+        reduce_bias,
+        second_gain,
+        second_shift,
+        start_vector,
+        end_vector,
+    ) = vector_at
 
     barrier = pltpu.get_barrier_semaphore()
 
@@ -170,14 +260,8 @@
     greet(core_dev)
     greet(x_dev)
     greet(y_dev)
-
-    @pl.when(zz > 0)
-    def _():
-        greet(down_dev)
-
-    @pl.when(zz < 3)
-    def _():
-        greet(up_dev)
+    for step in range(1, 4):
+        greet((lax.rem(dp + 4 * step, CHIPS), blk))
 
     @pl.when((blk == 1) & (dp < CHIPS - 1))
     def _():
@@ -191,6 +275,8 @@
 
     load_x.wait()
     load_wp.wait()
+    for copy in small:
+        copy.wait()
     for tile in range(3):
         cols = slice(256 * tile, 256 * tile + 256)
         q_part = project_cols(own_rows, 256 * tile, query_bias[:, cols])
@@ -202,9 +288,7 @@
             own_rows, 2 * WIDTH + 256 * tile, value_bias[:, cols]
         )
 
-    waits = 3 + (zz > 0).astype(jnp.int32) + (zz < 3).astype(jnp.int32)
-    waits = waits + ((blk == 0) & (dp > 0)).astype(jnp.int32)
-    pl.semaphore_wait(barrier, waits)
+    pl.semaphore_wait(barrier, 6 + ((blk == 0) & (dp > 0)).astype(jnp.int32))
 
     def to_core(at, src, dst):
         copy = pltpu.make_async_remote_copy(
@@ -221,7 +305,7 @@
     core_copies = []
     send_x = to_core(0, x_row.at[own_rows], x_row.at[own_rows])
     core_copies.append(send_x)
-    length = valid_length[0]
+    length, start_at, end_at, answered = (ref[...].reshape(1, 1) for ref in scalars)
     key_at = lax.broadcasted_iota(jnp.int32, (1, ROW), 1)
     key_live = key_at < length
     token_at = blk * BLOCK + lax.broadcasted_iota(jnp.int32, (BLOCK, 1), 0)
@@ -295,11 +379,13 @@
     centre = resid - row_mean(resid)
     scale_two = lax.rsqrt(row_mean(centre * centre) + norm_eps)
     normal = centre * scale_two
-    layer_output[...] = (normal * second_gain[...] + second_shift[...]).astype(LOW)
-
-    answered = answerable[0] > 0
-    start_slot = jnp.where(answered, start_index[0], 0)
-    end_slot = jnp.where(answered, end_index[0], 0)
+    out_own[...] = (normal * second_gain[...] + second_shift[...]).astype(LOW)
+    store_out = pltpu.make_async_copy(out_own, layer_output, out_sem.at[0])
+    store_out.start()
+
+    answered = answered > 0
+    start_slot = jnp.where(answered, start_at, 0)
+    end_slot = jnp.where(answered, end_at, 0)
     load_up.wait()
     cot = up[...].astype(FULL) * row_live
     cot = cot + (token_at == start_slot).astype(FULL) * start_vector[...]
@@ -353,96 +439,161 @@
             device_id_type=MESH,
         ).wait_send()
 
-    def base_of(plane, x_at, y_at):
-        return 24 * plane + 6 * (2 * y_at + x_at)
-
-    def first_sends(plane):
-        return (
-            (base_of(plane, 1 - xx, 1 - yy), 0, x_dev),
-            (base_of(plane, 1 - xx, 1 - yy) + 3, 2, y_dev),
-            (base_of(plane, 1 - xx, yy), 1, x_dev),
-            (base_of(plane, xx, 1 - yy) + 3, 3, y_dev),
+    def owner(plane, x_at, y_at):
+        return 4 * plane + 2 * y_at + x_at
+
+    def add_unit(chip, unit, arrivals):
+        value = grad[chip, unit].astype(FULL)
+        for arrival in arrivals:
+            value = value + arrival.astype(FULL)
+        grad[chip, unit] = value.astype(LOW)
+
+    def kept(plane):
+        return outer if plane in (0, 3) else jnp.logical_not(outer)
+
+    def taking_part(plane, third, step):
+        if third == 2:
+            pl.when(kept(plane))(step)
+        else:
+            step()
+
+    def pair_copy(plane):
+        return pltpu.make_async_remote_copy(
+            src_ref=grad.at[pl.ds(4 * plane, 4), pl.ds(4, 2)],
+            dst_ref=pair_in.at[plane // 2],
+            send_sem=pair_send.at[plane],
+            recv_sem=pair_recv.at[plane],
+            device_id=pair_dev,
+            device_id_type=MESH,
         )
 
-    def step_one(plane):
-        for first, slot, dev in first_sends(plane):
-            send(
-                grad.at[pl.ds(first, 3)],
-                plane_in.at[plane, slot],
-                s1_send.at[plane, slot],
-                s1_recv.at[plane, slot],
-                dev,
+    def first_copies(plane, third, slots=range(4)):
+        one, two = 2 * third, 2 * third + 1
+        return [
+            pltpu.make_async_remote_copy(
+                src_ref=grad.at[chip, unit],
+                dst_ref=first_in.at[plane, third, slot],
+                send_sem=first_send.at[plane, third, slot],
+                recv_sem=first_recv.at[plane, third, slot],
+                device_id=dev,
+                device_id_type=MESH,
             )
-
-    def second_sends(plane):
-        return (
-            (base_of(plane, xx, 1 - yy), 0, 0, y_dev),
-            (base_of(plane, 1 - xx, yy) + 3, 2, 1, x_dev),
+            for chip, unit, slot, dev in (
+                (owner(plane, 1 - xx, 1 - yy), one, 0, x_dev),
+                (owner(plane, 1 - xx, 1 - yy), two, 1, y_dev),
+                (owner(plane, 1 - xx, yy), one, 2, x_dev),
+                (owner(plane, xx, 1 - yy), two, 3, y_dev),
+            )
+            if slot in slots
+        ]
+
+    def second_copies(plane, third):
+        one, two = 2 * third, 2 * third + 1
+        return [
+            pltpu.make_async_remote_copy(
+                src_ref=grad.at[chip, unit],
+                dst_ref=second_in.at[plane, third, slot],
+                send_sem=second_send.at[plane, third, slot],
+                recv_sem=second_recv.at[plane, third, slot],
+                device_id=dev,
+                device_id_type=MESH,
+            )
+            for chip, unit, slot, dev in (
+                (owner(plane, xx, 1 - yy), one, 0, y_dev),
+                (owner(plane, 1 - xx, yy), two, 1, x_dev),
+            )
+        ]
+
+    def far_copy(plane, third):
+        slot = 6 if third == 2 else 3 * third + jnp.where(zz < plane, zz, zz - 1)
+        return pltpu.make_async_remote_copy(
+            src_ref=grad.at[owner(plane, xx, yy), pl.ds(2 * third, 2)],
+            dst_ref=far_in.at[slot],
+            send_sem=far_send.at[plane, third],
+            recv_sem=far_recv.at[slot],
+            device_id=(owner(plane, xx, yy), blk),
+            device_id_type=MESH,
         )
 
-    def add_units(first, arrays):
-        @pl.loop(0, 3)
-        def _(at):
-            value = grad[first + at].astype(FULL)
-            for array, index in arrays:
-                value = value + array[index + (at,)].astype(FULL)
-            grad[first + at] = value.astype(LOW)
-
-    def step_two(plane):
-        for first, slot, slot2, dev in second_sends(plane):
-            wait_recv(plane_in.at[plane, slot], s1_recv.at[plane, slot])
-            add_units(first, [(plane_in, (plane, slot))])
-            send(
-                grad.at[pl.ds(first, 3)],
-                plane_in2.at[plane, slot2],
-                s2_send.at[plane, slot2],
-                s2_recv.at[plane, slot2],
-                dev,
-            )
-
-    def step_three(plane):
-        own = base_of(plane, xx, yy)
-        for slot, slot2, first in ((1, 0, own), (3, 1, own + 3)):
-            wait_recv(plane_in.at[plane, slot], s1_recv.at[plane, slot])
-            wait_recv(plane_in2.at[plane, slot2], s2_recv.at[plane, slot2])
-            add_units(first, [(plane_in, (plane, slot)), (plane_in2, (plane, slot2))])
-
-    def chain(plane):
-        own = base_of(plane, xx, yy)
-        below = zz < plane
-        way = jnp.where(below, 0, 1)
-
-        @pl.when(zz != plane)
+    def pair_step(plane, third):
+        @pl.when(jnp.logical_not(kept(plane)))
         def _():
-            for half in range(2):
-                first = own + 3 * half
-
-                @pl.when((below & (zz > 0)) | (jnp.logical_not(below) & (zz < 3)))
-                def _():
-                    wait_recv(chain_in.at[way, plane, half], chain_recv.at[way, plane, half])
-                    add_units(first, [(chain_in, (way, plane, half))])
-
-                send(
-                    grad.at[pl.ds(first, 3)],
-                    chain_in.at[way, plane, half],
-                    chain_send.at[plane, half],
-                    chain_recv.at[way, plane, half],
-                    (jnp.where(below, dp + 4, dp - 4), blk),
+            pair_copy(plane).start()
+
+    def pair_add(plane, third):
+        @pl.when(kept(plane))
+        def _():
+            pair_copy(plane).wait_recv()
+
+            @pl.loop(0, 4)
+            def _(chip):
+                for unit in range(2):
+                    add_unit(4 * plane + chip, 4 + unit, [pair_in[plane // 2, chip, unit]])
+
+            for copy in first_copies(plane, third):
+                copy.start()
+
+    def first_step(plane, third):
+        for copy in first_copies(plane, third):
+            copy.start()
+
+    def second_step(plane, third):
+        def step():
+            firsts = first_copies(plane, third, (0, 1))
+            seconds = second_copies(plane, third)
+            for way in range(2):
+                chip = (owner(plane, xx, 1 - yy), owner(plane, 1 - xx, yy))[way]
+                firsts[way].wait_recv()
+                add_unit(chip, 2 * third + way, [first_in[plane, third, way]])
+                seconds[way].start()
+
+        taking_part(plane, third, step)
+
+    def third_step(plane, third):
+        def step():
+            firsts = first_copies(plane, third, (2, 3))
+            seconds = second_copies(plane, third)
+            for way in range(2):
+                firsts[way].wait_recv()
+                seconds[way].wait_recv()
+                add_unit(
+                    owner(plane, xx, yy),
+                    2 * third + way,
+                    [first_in[plane, third, 2 + way], second_in[plane, third, way]],
                 )
 
-        @pl.when(zz == plane)
-        def _():
-            for half in range(2):
-                ways = ([0] if plane > 0 else []) + ([1] if plane < 3 else [])
-                for one in ways:
-                    wait_recv(chain_in.at[one, plane, half], chain_recv.at[one, plane, half])
-
-                @pl.loop(0, 3)
-                def _(at):
-                    value = grad[own + 3 * half + at].astype(FULL)
-                    for one in ways:
-                        value = value + chain_in[one, plane, half, at].astype(FULL)
-                    total[3 * half + at] = value
+            @pl.when(zz != plane)
+            def _():
+                far_copy(plane, third).start()
+
+        taking_part(plane, third, step)
+
+    def finish_step(_, third):
+        slots = (6,) if third == 2 else (3 * third, 3 * third + 1, 3 * third + 2)
+        for slot in slots:
+            wait_recv(far_in.at[slot], far_recv.at[slot])
+        for way in range(2):
+            value = grad[dp, 2 * third + way].astype(FULL)
+            for slot in slots:
+                value = value + far_in[slot, way].astype(FULL)
+            total[2 * third + way] = value
+
+    steps = {
+        "pair": pair_step,
+        "add": pair_add,
+        "first": first_step,
+        "second": second_step,
+        "third": third_step,
+        "finish": finish_step,
+    }
+
+    def serve(after):
+        for what, plane, third in SCHEDULE.get(after, ()):
+            steps[what](plane, third)
+
+    def put_unit(at, rows, values):
+        chip, unit = (at // 6, at % 6) if isinstance(at, int) else (lax.div(at, 6), lax.rem(at, 6))
+        grad[chip, unit, rows, :] = values.astype(LOW)
 
     core_copies[3].wait_recv()
     core_copies[4].wait_recv()
@@ -454,15 +605,15 @@
         )
         for unit in range(8):
             for tile in range(3):
-                grad[64 + 8 * at + unit, 96 * tile : 96 * tile + 96, :] = part[
+                put_unit(64 + 8 * at + unit, slice(96 * tile, 96 * tile + 96), part[
                     96 * unit : 96 * unit + 96, LANES * tile : LANES * tile + LANES
-                ].astype(LOW)
+                ])
 
     @pl.loop(1, 4)
     def _(at):
         reduce_rows(at)
 
-    step_one(3)
+    serve("reduce")
     reduce_rows(0)
 
     @pl.loop(0, 6)
@@ -480,6 +631,7 @@
             ]
 
     core_copies.append(to_core(5, gexp_own.at[oth], gexp_oth))
+    serve("slopes")
     grad_mixed = resid_two[...]
     for half in range(2):
         grad_mixed = grad_mixed + dot_nt(
@@ -497,6 +649,8 @@
     put_bias(12, col_sum(pulled_low.astype(FULL)))
     core_copies.append(to_core(6, gbr_own.at[:, oth_384], gbr_oth))
 
+    serve("norm")
+
     core_copies[2].wait_recv()
     core_copies[5].wait_recv()
 
@@ -509,20 +663,19 @@
         rows = pl.ds(aligned(at * 48, 48), 48)
         for unit in range(32):
             piece = part[24 * unit : 24 * unit + 24, :]
-            grad[32 + unit, rows, :] = both(piece[:, :LANES], piece[:, LANES:]).astype(LOW)
-
-    step_one(2)
-
+            put_unit(32 + unit, rows, both(piece[:, :LANES], piece[:, LANES:]))
+
+    serve("expand")
     gatt[...] = dot_nt(gbr_own[...], wo[...]).astype(LOW)
     core_copies[1].wait_recv()
     core_copies[6].wait_recv()
     part = dot_tn(both(att_own[...], att_oth[...]), both(gbr_own[:, own_384], gbr_oth[...]))
     for unit in range(8):
         for tile in range(3):
-            grad[24 + unit, 96 * tile : 96 * tile + 96, :] = part[
+            put_unit(24 + unit, slice(96 * tile, 96 * tile + 96), part[
                 96 * unit : 96 * unit + 96, LANES * tile : LANES * tile + LANES
-            ].astype(LOW)
-    step_one(1)
+            ])
+    serve("output")
 
     qt[...] = q_own[...].T
     gat[...] = gatt[...].T
@@ -551,9 +704,13 @@
             slope[at : at + HEAD_DIM, slot] = dot_nn(gat[rows, :], soft_low).astype(LOW)
         gpj_own[:, cols] = (grad_query * HEAD_DIM ** (-0.5)).astype(LOW)
 
-    @pl.loop(0, HEADS // 2)
-    def _(pair):
-        head_pair(pair)
+    for part in range(3):
+
+        @pl.loop(2 * part, 2 * part + 2)
+        def _(pair):
+            head_pair(pair)
+
+        serve("heads" + str(part))
 
     def turned(pair, block, first):
         lanes = pl.ds(aligned(pair * ROW + block * BLOCK, BLOCK), BLOCK)
@@ -564,7 +721,6 @@
             at = pair * LANES + first * (WIDTH // LANES)
             dkv_out[:, at : at + LANES] = turned(pair, oth, first)
     core_copies.append(to_core(7, dkv_out, dkv_in))
-    step_two(3)
     core_copies[7].wait_recv()
     for pair in range(HEADS // 2):
         for first in (0, LANES):
@@ -572,12 +728,16 @@
             gpj_own[:, WIDTH + at : WIDTH + at + LANES] = (
                 turned(pair, blk, first).astype(FULL) + dkv_in[:, at : at + LANES].astype(FULL)
             ).astype(LOW)
+    serve("keys")
     own_1152 = pl.ds(aligned(blk * 1152, 1152), 1152)
     oth_1152 = pl.ds(aligned(oth * 1152, 1152), 1152)
     core_copies.append(to_core(8, gpj_own.at[:, oth_1152], gpj_oth))
     put_bias(0, col_sum(gpj_own[:, :WIDTH].astype(FULL)))
     put_bias(6, col_sum(gpj_own[:, 2 * WIDTH :].astype(FULL)))
-    input_gradient[...] = (resid_one[...] + dot_nt(gpj_own[...], wp[...])).astype(LOW)
+
+    def input_gradient_part():
+        gin_own[...] = (resid_one[...] + dot_nt(gpj_own[...], wp[...])).astype(LOW)
+        pltpu.make_async_copy(gin_own, input_gradient, out_sem.at[1]).start()
 
     core_copies[8].wait_recv()
 
@@ -591,92 +751,120 @@
         for unit in range(24):
             for tile in range(3):
                 rows = pl.ds(aligned(at * 96 + 32 * tile, 32), 32)
-                grad[unit, rows, :] = part[
+                put_unit(unit, rows, part[
                     32 * unit : 32 * unit + 32, LANES * tile : LANES * tile + LANES
-                ].astype(LOW)
-
-    step_one(0)
-
-    def bias_hop(at, here, there, dev):
+                ])
+
+    serve("project")
+    input_gradient_part()
+    serve("input")
+
+    def bias_leaves(at, here, dev):
         @pl.when(here)
         def _():
             send(bias_sum, bias_in.at[at], bias_send.at[0], bias_recv.at[at], dev)
 
+    def bias_comes(at, there):
         @pl.when(there)
         def _():
             wait_recv(bias_in.at[at], bias_recv.at[at])
             bias_sum[...] += bias_in[at]
 
-    bias_hop(0, xx == 0, xx == 1, x_dev)
-    step_two(2)
-    step_three(3)
-    chain(3)
-    bias_hop(1, (xx == 1) & (yy == 0), (xx == 1) & (yy == 1), y_dev)
-    step_two(1)
-    step_three(2)
-    chain(2)
     corner = (xx == 1) & (yy == 1)
-
-    @pl.when(corner & (zz > 0))
-    def _():
-        wait_recv(bias_in.at[2], bias_recv.at[2])
-        bias_sum[...] += bias_in[2]
+    last = dp == CHIPS - 1
+    bias_leaves(0, xx == 0, x_dev)
+    serve("bias0")
+    bias_comes(0, xx == 1)
+    bias_leaves(1, (xx == 1) & (yy == 0), y_dev)
+    serve("bias1")
+    bias_comes(1, corner)
 
     @pl.when(corner & (zz < 3))
     def _():
-        send(bias_sum, bias_in.at[2], bias_send.at[0], bias_recv.at[2], up_dev)
-
-    step_two(0)
-    step_three(1)
-    chain(1)
-    last = dp == CHIPS - 1
+        send(
+            bias_sum,
+            bias_in.at[2 + zz],
+            bias_send.at[0],
+            bias_recv.at[2 + zz],
+            (CHIPS - 1, blk),
+        )
+
+    serve("bias2")
+
+    @pl.when(last)
+    def _():
+        for at in range(2, 5):
+            wait_recv(bias_in.at[at], bias_recv.at[at])
+            bias_sum[...] += bias_in[at]
 
     @pl.when(last & (blk == 0))
     def _():
-        send(bias_sum, bias_in.at[3], bias_send.at[0], bias_recv.at[3], core_dev)
+        send(bias_sum, bias_in.at[5], bias_send.at[0], bias_recv.at[5], core_dev)
+
+    serve("bias3")
 
     @pl.when(last & (blk == 1))
     def _():
-        wait_recv(bias_in.at[3], bias_recv.at[3])
-        flat[1728:1800, :] = bias_sum[...] + bias_in[3]
-
-    step_three(0)
-    chain(0)
-
-    last_send = to_core(9, total.at[pl.ds(3 * oth, 3)], total_oth)
-    core_copies.append(last_send)
-
-    def lay_out(source, first, column_half):
-        for unit in range(3):
-            kind_at = 3 * device + unit
-            kinds = (
-                (kind_at < 24, 32, 9),
-                (((kind_at >= 24) & (kind_at < 32)) | (kind_at >= 64), 96, 3),
-                ((kind_at >= 32) & (kind_at < 64), 24, 12),
-            )
-            for fits, rows, tiles in kinds:
-
-                @pl.when(fits)
-                def _():
-                    for tile in range(tiles):
-                        for group in range(rows // 8):
-                            at = rows * tile + 8 * group
-                            to = 576 * unit + 16 * group * tiles + tile + column_half * tiles
-                            flat[pl.ds(to, 8, stride=2 * tiles), :] = source[
-                                first + unit, at : at + 8, :
-                            ]
-
-    lay_out(total, 3 * blk, blk)
-    last_send.wait_recv()
-    lay_out(total_oth, 0, oth)
+        wait_recv(bias_in.at[5], bias_recv.at[5])
+        flat[1728:1800, :] = bias_sum[...] + bias_in[5]
+
+    def lay_out(source, first, column_half, unit):
+        kind_at = 3 * device + unit
+        kinds = (
+            (kind_at < 24, 32, 9),
+            (((kind_at >= 24) & (kind_at < 32)) | (kind_at >= 64), 96, 3),
+            ((kind_at >= 32) & (kind_at < 64), 24, 12),
+        )
+        for fits, rows, tiles in kinds:
+
+            @pl.when(fits)
+            def _():
+                for tile in range(tiles):
+                    for group in range(rows // 8):
+                        at = rows * tile + 8 * group
+                        to = 576 * unit + 16 * group * tiles + tile + column_half * tiles
+                        flat[pl.ds(to, 8, stride=2 * tiles), :] = source[
+                            first + unit, at : at + 8, :
+                        ]
+
+    def to_core_when(at, here, src, dst):
+        @pl.when(here)
+        def _():
+            send(src, dst, core_send.at[at], core_recv.at[at], core_dev)
+
+    serve("end0")
+    to_core_when(9, blk == 1, total.at[pl.ds(0, 3)], total_oth)
+    to_core_when(10, blk == 0, total.at[pl.ds(3, 1)], total_oth.at[pl.ds(0, 1)])
 
     @pl.when(blk == 1)
     def _():
+        lay_out(total, 3, 1, 0)
+        wait_recv(total_oth.at[pl.ds(0, 1)], core_recv.at[10])
+        lay_out(total_oth, 0, 0, 0)
         send(flat.at[0:72], flat.at[1728:1800], fix_send.at[0], fix_recv.at[0], core_dev)
 
-    @pl.when((blk == 0) & (dp > 0))
+    @pl.when(blk == 0)
     def _():
-        send(flat.at[0:72], flat.at[1728:1800], fix_send.at[0], fix_recv.at[0], (dp - 1, 1))
+        for unit in range(3):
+            lay_out(total, 0, 0, unit)
+        wait_recv(total_oth, core_recv.at[9])
+        for unit in range(3):
+            lay_out(total_oth, 0, 1, unit)
+
+        @pl.when(dp > 0)
+        def _():
+            send(flat.at[0:72], flat.at[1728:1800], fix_send.at[0], fix_recv.at[0], (dp - 1, 1))
+
+    serve("end1")
+    to_core_when(11, blk == 0, total.at[pl.ds(4, 2)], total_oth.at[pl.ds(1, 2)])
+
+    @pl.when(blk == 1)
+    def _():
+        for unit in range(1, 3):
+            lay_out(total, 3, 1, unit)
+        wait_recv(total_oth.at[pl.ds(1, 2)], core_recv.at[11])
+        for unit in range(1, 3):
+            lay_out(total_oth, 0, 0, unit)
 
     @pl.when(device < 2 * CHIPS - 1)
     def _():
@@ -691,20 +879,40 @@
         rows = at * 56
         first = pltpu.roll(flat[pl.ds(rows + skip, 56), :], LANES - shift, 1)
         second = pltpu.roll(flat[pl.ds(rows + skip + 1, 56), :], LANES - shift, 1)
-        grads[pl.ds(aligned(rows, 8), 56), :] = jnp.where(stays, first, second)
+        placed[pl.ds(aligned(rows, 8), 56), :] = jnp.where(stays, first, second)
+
+    store_grads = pltpu.make_async_copy(placed, grads, out_sem.at[2])
+    store_grads.start()
 
     for copy in core_copies:
         copy.wait_send()
+
+    @pl.when(blk == 1)
+    def _():
+        wait_send(total.at[pl.ds(0, 3)], core_send.at[9])
+
+    @pl.when(blk == 0)
+    def _():
+        wait_send(total.at[pl.ds(3, 1)], core_send.at[10])
+        wait_send(total.at[pl.ds(4, 2)], core_send.at[11])
+
     for plane in range(4):
-        for slot in range(4):
-            wait_send(plane_in.at[plane, slot], s1_send.at[plane, slot])
-        for slot in range(2):
-            wait_send(plane_in2.at[plane, slot], s2_send.at[plane, slot])
-
-        @pl.when(zz != plane)
+
+        @pl.when(jnp.logical_not(kept(plane)))
         def _():
-            for half in range(2):
-                wait_send(chain_in.at[0, plane, half], chain_send.at[plane, half])
+            pair_copy(plane).wait_send()
+
+        for third in range(3):
+
+            def sent():
+                for copy in first_copies(plane, third) + second_copies(plane, third):
+                    copy.wait_send()
+
+                @pl.when(zz != plane)
+                def _():
+                    far_copy(plane, third).wait_send()
+
+            taking_part(plane, third, sent)
 
     @pl.when(jnp.logical_not(last & (blk == 1)))
     def _():
@@ -713,6 +921,25 @@
     @pl.when(device > 0)
     def _():
         wait_send(flat.at[0:72], fix_send.at[0])
+
+    store_out.wait()
+    pltpu.make_async_copy(gin_own, input_gradient, out_sem.at[1]).wait()
+    store_grads.wait()
+
+
+def hand_over(*refs):
+    sources, targets, held, sems = refs[:3], refs[3:6], refs[6:9], refs[9]
+    reads = [pltpu.make_async_copy(*pair, sems.at[at]) for at, pair in enumerate(zip(sources, held))]
+    writes = [
+        pltpu.make_async_copy(*pair, sems.at[3 + at]) for at, pair in enumerate(zip(held, targets))
+    ]
+    for read in reads:
+        read.start()
+    for read, write in zip(reads, writes):
+        read.wait()
+        write.start()
+    for write in writes:
+        write.wait()
 
 
 def fused_layer(
@@ -739,26 +966,22 @@
     end_index,
     answerable,
 ):
-    vectors = [
-        vector.reshape(1, -1)
-        for vector in (
-            query_bias,
-            value_bias,
-            output_bias,
-            first_gain,
-            first_shift,
-            expand_bias,
-            reduce_bias,
-            second_gain,
-            second_shift,
-            start_vector,
-            end_vector,
-        )
-    ]
-    scalars = [valid_length, start_index, end_index, answerable]
+    vectors = (
+        query_bias,
+        value_bias,
+        output_bias,
+        first_gain,
+        first_shift,
+        expand_bias,
+        reduce_bias,
+        second_gain,
+        second_shift,
+        start_vector,
+        end_vector,
+    )
+    scalars = (valid_length, start_index, end_index, answerable)
     anywhere = pl.BlockSpec(memory_space=pl.ANY)
     in_vmem = pl.BlockSpec(memory_space=pltpu.VMEM)
-    in_smem = pl.BlockSpec(memory_space=pltpu.SMEM)
 
     def low(*shape):
         return pltpu.VMEM(shape, LOW)
@@ -775,6 +998,7 @@
         low(HEADS, BLOCK, ROW),
         low(BLOCK, WIDTH),
         low(ROW, WIDTH),
+        tuple(full(1, vector.shape[0]) for vector in vectors),
         low(BLOCK, WIDTH),
         low(ROW, WIDTH),
         low(ROW, WIDTH),
@@ -803,38 +1027,47 @@
         low(BLOCK, 3 * WIDTH),
         low(BLOCK, 3 * WIDTH // 2),
         full(BLOCK, ROW),
-        low(96, UNIT, LANES),
-        low(4, 4, 3, UNIT, LANES),
-        low(4, 2, 3, UNIT, LANES),
-        low(2, 4, 2, 3, UNIT, LANES),
+        low(BLOCK, WIDTH),
+        low(BLOCK, WIDTH),
+        low(CHIPS, 6, UNIT, LANES),
+        low(2, 4, 2, UNIT, LANES),
+        low(4, 3, 4, UNIT, LANES),
+        low(4, 3, 2, UNIT, LANES),
+        low(7, 2, UNIT, LANES),
         full(6, UNIT, LANES),
         full(3, UNIT, LANES),
         full(1816, LANES),
+        full(1736, LANES),
         full(72, LANES),
-        full(4, 72, LANES),
+        full(6, 72, LANES),
         dma((7,)),
-        dma((10,)),
-        dma((10,)),
-        dma((4, 4)),
-        dma((4, 4)),
-        dma((4, 2)),
-        dma((4, 2)),
-        dma((4, 2)),
-        dma((2, 4, 2)),
+        dma((len(vectors),)),
+        dma((12,)),
+        dma((12,)),
+        dma((4,)),
+        dma((4,)),
+        dma((4, 3, 4)),
+        dma((4, 3, 4)),
+        dma((4, 3, 2)),
+        dma((4, 3, 2)),
+        dma((4, 3)),
+        dma((7,)),
         dma((1,)),
-        dma((4,)),
+        dma((6,)),
         dma((1,)),
         dma((1,)),
+        dma((3,)),
     ]
-    layer_output, input_gradient, grads = pl.pallas_call(
+    results = (
+        jax.ShapeDtypeStruct((BLOCK, WIDTH), LOW),
+        jax.ShapeDtypeStruct((BLOCK, WIDTH), LOW),
+        jax.ShapeDtypeStruct((1736, LANES), FULL),
+    )
+    made = pl.pallas_call(
         layer_kernel,
-        out_shape=(
-            jax.ShapeDtypeStruct((BLOCK, WIDTH), LOW),
-            jax.ShapeDtypeStruct((BLOCK, WIDTH), LOW),
-            jax.ShapeDtypeStruct((1736, LANES), FULL),
-        ),
-        in_specs=[anywhere] * 7 + [in_vmem] * len(vectors) + [in_smem] * 4,
-        out_specs=(in_vmem, in_vmem, in_vmem),
+        out_shape=results,
+        in_specs=[anywhere] * 7 + [(anywhere,) * len(vectors), (in_vmem,) * len(scalars)],
+        out_specs=(anywhere,) * 3,
         scratch_shapes=scratch,
         compiler_params=pltpu.CompilerParams(
             collective_id=0, has_side_effects=True, vmem_limit_bytes=63 * 2**20
@@ -848,13 +1081,21 @@
         output_weight,
         expand_weight,
         reduce_weight,
-        *vectors,
-        *scalars,
-    )
+        vectors,
+        scalars,
+    )
+    layer_output, input_gradient, grads = pl.pallas_call(
+        hand_over,
+        out_shape=results,
+        in_specs=[anywhere] * 3,
+        out_specs=(anywhere,) * 3,
+        scratch_shapes=[pltpu.VMEM(result.shape, result.dtype) for result in results] + [dma((6,))],
+        name="hand_over",
+    )(*made)
     return (
         layer_output.reshape(1, BLOCK, WIDTH),
         input_gradient.reshape(1, BLOCK, WIDTH),
-        grads.reshape(-1)[: 96 * 3 * 576 * LANES // 96 + 288],
+        grads.reshape(-1)[: 3 * 2 * UNIT * LANES + UNIT],
     )
 
 

time: 161 us -> 110 us (0.68)
  the two profiles are of different devices: /device:TPU:1 before, /device:TPU:17 now
where the time goes in v2:
time: 110 us; the launch traced here: 109 us
  Pallas kernels  106 us (96%)
  between operations  3.39 us (3%)
    pallas_call x1, Pallas kernels, fused_layer(): pl.pallas_call(layer_kernel, out_shape=results, in_specs=[anywhere] * 7 +...  104 us
    pallas_call x1, Pallas kernels, fused_layer(): pl.pallas_call(hand_over, out_shape=results, in_specs=[anywhere] * 3, out...  2.38 us

profile of v2, /device:TPU:17, one launch (start us, length us, event | category | flops | bytes accessed | tf_op | source)
XLA Modules:
  0.0 109.4 jit_solution(6335279553358312574)
XLA Ops:
  3.2 103.6 %encoder_layer.1 = (bf16[256,768]{1,0:T(8,128)(2,1)}, bf16[256,768]{1,0:T(8,128)(2,1)}, f32[1736,128]{1,0:T(8,128)}) custom-call(bf16[256,768]{1,0:T(8,128)(2,1)} %bitcast.8, bf16[256,768]{1,0:T(8,128)(2,1)} %bitcast.9, bf16[12,256,512]{2,1,0:T(8,128)(2,1)} %bitcast.7, bf16[768,2304]{1,0:T(8,128)(2,1)} %w_project.1, bf16[768,768]{1,0:T(8,128)(2,1)} %w_output.1, ...), custom_call_target="tpu_custom_call" | custom-call | tf_op jit(solution)/shard_map/encoder_layer/pallas_call | solution.py:1066
  106.9 2.4 %hand_over.1 = (bf16[256,768]{1,0:T(8,128)(2,1)}, bf16[256,768]{1,0:T(8,128)(2,1)}, f32[1736,128]{1,0:T(8,128)}) custom-call(bf16[256,768]{1,0:T(8,128)(2,1)} %get-tuple-element.9.refs_0_, bf16[256,768]{1,0:T(8,128)(2,1)} %get-tuple-element.10.refs_1_, f32[1736,128]{1,0:T(8,128)} %get-tuple-element.11.refs_2_), custom_call_target="tpu_custom_call" | custom-call | tf_op jit(solution)/shard_map/hand_over/pallas_call | solution.py:1087

commit v3 on v2

--- a/solution.py
+++ b/solution.py
@@ -47,71 +47,83 @@
 
 
 SCHEDULE = {
-    "reduce": (
+    "reduce0": (
+        ("first", 3, 0),
+    ),
+    "reduce1": (
         ("first", 3, 1),
     ),
+    "reduce2": (
+        ("pair", 3, 2),
+    ),
     "slopes": (
-        ("first", 3, 0),
+        ("second", 3, 0),
     ),
     "norm": (
         ("second", 3, 1),
     ),
-    "expand": (
-        ("pair", 2, 2),
-        ("pair", 3, 2),
-        ("second", 3, 0),
-    ),
     "output": (
+        ("pair", 1, 2),
         ("first", 1, 1),
     ),
     "heads0": (
         ("first", 1, 0),
     ),
+    "heads1": (
+        ("third", 3, 1),
+        ("second", 1, 1),
+        ("first", 2, 1),
+    ),
     "heads2": (
-        ("second", 1, 1),
-        ("first", 2, 0),
+        ("third", 3, 0),
+        ("pair", 2, 2),
     ),
     "keys": (
-        ("pair", 1, 2),
+        ("second", 1, 0),
     ),
     "project": (
         ("first", 0, 0),
-        ("pair", 0, 2),
+        ("first", 0, 1),
+    ),
+    "input": (
+        ("second", 0, 0),
+    ),
+    "bias0": (
+        ("first", 0, 2),
+        ("chain", 3, 1),
+        ("second", 0, 1),
+        ("third", 1, 1),
         ("add", 3, 2),
+        ("second", 2, 1),
+        ("chain", 3, 0),
+        ("third", 0, 0),
+        ("third", 1, 0),
+    ),
+    "bias1": (
+        ("second", 0, 2),
         ("second", 3, 2),
+        ("first", 2, 0),
+    ),
+    "bias2": (
+        ("add", 1, 2),
+        ("third", 0, 1),
+        ("add", 2, 2),
+        ("third", 2, 1),
+        ("third", 0, 2),
+        ("third", 3, 2),
+        ("chain", 0, 0),
+    ),
+    "bias3": (
         ("second", 2, 0),
-        ("third", 3, 1),
-    ),
-    "bias0": (
-        ("second", 0, 0),
-        ("first", 0, 1),
-        ("third", 3, 0),
-        ("second", 1, 0),
-        ("third", 1, 1),
-        ("add", 2, 2),
-    ),
-    "bias1": (
-        ("third", 0, 0),
-        ("second", 0, 1),
+        ("second", 1, 2),
+        ("second", 2, 2),
+        ("chain", 0, 1),
         ("third", 2, 0),
-        ("add", 0, 2),
-        ("first", 2, 1),
-        ("third", 3, 2),
-    ),
-    "bias2": (
-        ("third", 1, 0),
-        ("third", 0, 1),
-        ("second", 0, 2),
-        ("second", 2, 1),
-        ("add", 1, 2),
-        ("second", 1, 2),
-    ),
-    "bias3": (
-        ("third", 0, 2),
-        ("third", 2, 1),
-        ("second", 2, 2),
+        ("chain", 0, 2),
+        ("third", 1, 2),
         ("third", 2, 2),
-        ("third", 1, 2),
+    ),
+    "end0": (
         ("finish", 0, 0),
         ("finish", 0, 1),
     ),
@@ -119,6 +131,8 @@
         ("finish", 0, 2),
     ),
 }
+PAIRED = (0, 1, 1, 1)
+CHAINED = (True, False, False, True)
 
 
 def aligned(start, step):
@@ -212,7 +226,6 @@
     yy = (dp // 2) % 2
     zz = dp // 4
     column = dp % 4
-    outer = (zz == 0) | (zz == 3)
     core_dev = (dp, oth)
     x_dev = (dp + 1 - 2 * xx, blk)
     y_dev = (dp + 2 - 4 * yy, blk)
@@ -227,17 +240,15 @@
     own_rows = pl.ds(aligned(blk * BLOCK, BLOCK), BLOCK)
     oth_rows = pl.ds(aligned(oth * BLOCK, BLOCK), BLOCK)
     load_x = load(0, hidden, x_row.at[own_rows])
-    load_wp = load(1, w_project, wp)
+    load_wp = [
+        load(6 + part, w_project.at[:, part_cols], wp.at[:, part_cols])
+        for part, part_cols in enumerate(pl.ds(WIDTH * part, WIDTH) for part in range(3))
+    ]
     small = []
     for at, (src, dst) in enumerate(zip(vectors, vector_at)):
         small.append(pltpu.make_async_copy(src, dst.at[0], vector_sem.at[at]))
     for copy in small:
         copy.start()
-    load_wo = load(2, w_output, wo)
-    load_we = load(3, w_expand, we)
-    load_wr = load(4, w_reduce, wr)
-    load_up = load(5, upstream, up)
-    load_te = load(6, teacher, te)
     (
         query_bias,
         value_bias,
@@ -267,29 +278,6 @@
     def _():
         greet((dp + 1, 0))
 
-    def project_cols(rows, at, bias):
-        part = dot_nn(x_row[rows, :], wp[:, pl.ds(at, 256)])
-        if bias is not None:
-            part = part + bias
-        return part.astype(LOW)
-
-    load_x.wait()
-    load_wp.wait()
-    for copy in small:
-        copy.wait()
-    for tile in range(3):
-        cols = slice(256 * tile, 256 * tile + 256)
-        q_part = project_cols(own_rows, 256 * tile, query_bias[:, cols])
-        q_own[:, cols] = q_part * jnp.asarray(HEAD_DIM ** (-0.5), LOW)
-    for tile in range(3):
-        cols = slice(256 * tile, 256 * tile + 256)
-        k_row[own_rows, cols] = project_cols(own_rows, WIDTH + 256 * tile, None)
-        v_row[own_rows, cols] = project_cols(
-            own_rows, 2 * WIDTH + 256 * tile, value_bias[:, cols]
-        )
-
-    pl.semaphore_wait(barrier, 6 + ((blk == 0) & (dp > 0)).astype(jnp.int32))
-
     def to_core(at, src, dst):
         copy = pltpu.make_async_remote_copy(
             src_ref=src,
@@ -302,15 +290,34 @@
         copy.start()
         return copy
 
-    core_copies = []
-    send_x = to_core(0, x_row.at[own_rows], x_row.at[own_rows])
-    core_copies.append(send_x)
+    load_x.wait()
+    pl.semaphore_wait(barrier, 6 + ((blk == 0) & (dp > 0)).astype(jnp.int32))
+    core_copies = [to_core(0, x_row.at[own_rows], x_row.at[own_rows])]
+
     length, start_at, end_at, answered = (ref[...].reshape(1, 1) for ref in scalars)
     key_at = lax.broadcasted_iota(jnp.int32, (1, ROW), 1)
     key_live = key_at < length
     token_at = blk * BLOCK + lax.broadcasted_iota(jnp.int32, (BLOCK, 1), 0)
     row_live = (token_at < length).astype(FULL)
     live_map[...] = jnp.where(key_live, 1.0 / ROW, 0.0) * row_live
+
+    def project(rows, part):
+        return dot_nn(x_row[rows, :], wp[:, WIDTH * part : WIDTH * part + WIDTH])
+
+    load_wp[0].wait()
+    for copy in small:
+        copy.wait()
+    own_queries = (project(own_rows, 0) + query_bias[...]).astype(LOW)
+    q_own[...] = own_queries * jnp.asarray(HEAD_DIM ** (-0.5), LOW)
+    load_wp[1].wait()
+    load_wo = load(1, w_output, wo)
+    load_we = load(2, w_expand, we)
+    load_wr = load(3, w_reduce, wr)
+    load_up = load(4, upstream, up)
+    load_te = load(5, teacher, te)
+    k_row[own_rows, :] = project(own_rows, 1).astype(LOW)
+    load_wp[2].wait()
+    v_row[own_rows, :] = (project(own_rows, 2) + value_bias[...]).astype(LOW)
     pltpu.make_async_remote_copy(
         src_ref=x_row.at[oth_rows],
         dst_ref=x_row.at[oth_rows],
@@ -319,35 +326,43 @@
         device_id=core_dev,
         device_id_type=MESH,
     ).wait_recv()
-    for tile in range(3):
-        cols = slice(256 * tile, 256 * tile + 256)
-        k_row[oth_rows, cols] = project_cols(oth_rows, WIDTH + 256 * tile, None)
-        v_row[oth_rows, cols] = project_cols(
-            oth_rows, 2 * WIDTH + 256 * tile, value_bias[:, cols]
-        )
+    k_row[oth_rows, :] = project(oth_rows, 1).astype(LOW)
+    v_row[oth_rows, :] = (project(oth_rows, 2) + value_bias[...]).astype(LOW)
 
     lane = lax.broadcasted_iota(jnp.int32, (1, LANES), 1)
     head_lanes = ((lane < HEAD_DIM).astype(LOW), (lane >= HEAD_DIM).astype(LOW))
 
-    @pl.loop(0, HEADS // 2)
-    def _(pair):
-        cols = pl.ds(aligned(pair * LANES, LANES), LANES)
-        q_pair = q_own[:, cols]
-        k_pair = k_row[:, cols]
-        v_pair = v_row[:, cols]
-        gathered = None
-        for side in range(2):
-            scores = dot_nt(q_pair * head_lanes[side], k_pair)
-            scores = jnp.where(key_live, scores, -1e30)
-            peak = jnp.max(scores, axis=-1, keepdims=True)
-            terms = jnp.exp(scores - peak)
-            scale = 1.0 / jnp.sum(terms, axis=-1, keepdims=True)
-            soft_low = (terms * scale).astype(LOW)
-            soft[2 * pair + side] = soft_low
-            part = dot_nn(soft_low, v_pair * head_lanes[side])
-            gathered = part if gathered is None else gathered + part
-        att_own[:, cols] = gathered.astype(LOW)
-
+    def pair_cols(head):
+        return slice(LANES * (head // 2), LANES * (head // 2) + LANES)
+
+    def head_scores(head):
+        cols = pair_cols(head)
+        scores = dot_nt(q_own[:, cols] * head_lanes[head % 2], k_row[:, cols])
+        return jnp.where(key_live, scores, -1e30)
+
+    def head_soft(scores):
+        peak = jnp.max(scores, axis=-1, keepdims=True)
+        terms = jnp.exp(scores - peak)
+        scale = 1.0 / jnp.sum(terms, axis=-1, keepdims=True)
+        return (terms * scale).astype(LOW)
+
+    gathered = {}
+
+    def head_gather(head):
+        cols = pair_cols(head)
+        gathered[head] = dot_nn(soft[head], v_row[:, cols] * head_lanes[head % 2])
+        if head % 2 == 1:
+            att_own[:, cols] = (gathered[head - 1] + gathered[head]).astype(LOW)
+
+    ahead = head_scores(0)
+    for head in range(HEADS):
+        scores = ahead
+        if head + 1 < HEADS:
+            ahead = head_scores(head + 1)
+        if head > 0:
+            head_gather(head - 1)
+        soft[head] = head_soft(scores)
+    head_gather(HEADS - 1)
     core_copies.append(to_core(1, att_own, att_oth))
 
     load_wo.wait()
@@ -362,7 +377,7 @@
 
     load_we.wait()
 
-    @pl.loop(0, 6)
+    @pl.loop(0, 6, unroll=6)
     def _(at):
         cols = pl.ds(aligned(at * 512, 512), 512)
         expanded = dot_nn(mix_own[...], we[:, cols]) + expand_bias[:, cols]
@@ -448,21 +463,24 @@
             value = value + arrival.astype(FULL)
         grad[chip, unit] = value.astype(LOW)
 
+    def paired(plane, third):
+        return third >= 3 - PAIRED[plane]
+
     def kept(plane):
-        return outer if plane in (0, 3) else jnp.logical_not(outer)
+        return (lax.rem(zz, 2) == 0) if plane < 2 else (lax.rem(zz, 2) == 1)
 
     def taking_part(plane, third, step):
-        if third == 2:
+        if paired(plane, third):
             pl.when(kept(plane))(step)
         else:
             step()
 
-    def pair_copy(plane):
+    def pair_copy(plane, third):
         return pltpu.make_async_remote_copy(
-            src_ref=grad.at[pl.ds(4 * plane, 4), pl.ds(4, 2)],
-            dst_ref=pair_in.at[plane // 2],
-            send_sem=pair_send.at[plane],
-            recv_sem=pair_recv.at[plane],
+            src_ref=grad.at[pl.ds(4 * plane, 4), pl.ds(2 * third, 2)],
+            dst_ref=pair_in.at[plane % 2, 2 - third],
+            send_sem=pair_send.at[plane, third],
+            recv_sem=pair_recv.at[plane, third],
             device_id=pair_dev,
             device_id_type=MESH,
         )
@@ -504,31 +522,52 @@
             )
         ]
 
-    def far_copy(plane, third):
-        slot = 6 if third == 2 else 3 * third + jnp.where(zz < plane, zz, zz - 1)
+    def chained(plane, third):
+        return CHAINED[plane] and not paired(plane, third)
+
+    def last_slot(third, source, way):
+        return 6 * third + 2 * source + way
+
+    def passing_slot(plane, third, way):
+        return 18 + 6 * sum(CHAINED[:plane]) + 2 * third + way
+
+    def far_copy(plane, third, way):
+        below = zz < plane
+        if chained(plane, third):
+            target = jnp.where(below, dp + 4, dp - 4)
+            ends = jnp.where(below, zz + 1, zz - 1) == plane
+            passing = passing_slot(plane, third, way)
+            slot = jnp.where(ends, last_slot(third, jnp.where(below, 0, 1), way), passing)
+        else:
+            target = owner(plane, xx, yy)
+            slot = last_slot(third, jnp.where(below, zz, zz - 1), way)
         return pltpu.make_async_remote_copy(
-            src_ref=grad.at[owner(plane, xx, yy), pl.ds(2 * third, 2)],
+            src_ref=grad.at[owner(plane, xx, yy), 2 * third + way],
             dst_ref=far_in.at[slot],
-            send_sem=far_send.at[plane, third],
+            send_sem=far_send.at[plane, third, way],
             recv_sem=far_recv.at[slot],
-            device_id=(owner(plane, xx, yy), blk),
+            device_id=(target, blk),
             device_id_type=MESH,
         )
 
     def pair_step(plane, third):
         @pl.when(jnp.logical_not(kept(plane)))
         def _():
-            pair_copy(plane).start()
+            pair_copy(plane, third).start()
 
     def pair_add(plane, third):
         @pl.when(kept(plane))
         def _():
-            pair_copy(plane).wait_recv()
+            pair_copy(plane, third).wait_recv()
 
             @pl.loop(0, 4)
             def _(chip):
-                for unit in range(2):
-                    add_unit(4 * plane + chip, 4 + unit, [pair_in[plane // 2, chip, unit]])
+                for way in range(2):
+                    add_unit(
+                        4 * plane + chip,
+                        2 * third + way,
+                        [pair_in[plane % 2, 2 - third, chip, way]],
+                    )
 
             for copy in first_copies(plane, third):
                 copy.start()
@@ -561,22 +600,44 @@
                     2 * third + way,
                     [first_in[plane, third, 2 + way], second_in[plane, third, way]],
                 )
-
-            @pl.when(zz != plane)
+                leaves = (zz == 0) | (zz == 3) if chained(plane, third) else zz >= 0
+
+                @pl.when((zz != plane) & leaves)
+                def _():
+                    far_copy(plane, third, way).start()
+
+        taking_part(plane, third, step)
+
+    def chain_step(plane, third):
+        @pl.when((zz != plane) & (zz > 0) & (zz < 3))
+        def _():
+            for way in range(2):
+                slot = passing_slot(plane, third, way)
+                wait_recv(far_in.at[slot], far_recv.at[slot])
+                add_unit(owner(plane, xx, yy), 2 * third + way, [far_in[slot]])
+                far_copy(plane, third, way).start()
+
+    def finish_step(_, third):
+        for plane in range(4):
+            if paired(plane, third):
+                sources = [z for z in range(4) if z != plane and (z % 2 == 0) == (plane < 2)]
+                sources = [z if z < plane else z - 1 for z in sources]
+            elif CHAINED[plane]:
+                sources = ([0] if plane > 0 else []) + ([1] if plane < 3 else [])
+            else:
+                sources = [0, 1, 2]
+
+            @pl.when(zz == plane)
             def _():
-                far_copy(plane, third).start()
-
-        taking_part(plane, third, step)
-
-    def finish_step(_, third):
-        slots = (6,) if third == 2 else (3 * third, 3 * third + 1, 3 * third + 2)
-        for slot in slots:
-            wait_recv(far_in.at[slot], far_recv.at[slot])
-        for way in range(2):
-            value = grad[dp, 2 * third + way].astype(FULL)
-            for slot in slots:
-                value = value + far_in[slot, way].astype(FULL)
-            total[2 * third + way] = value
+                for way in range(2):
+                    slots = [last_slot(third, source, way) for source in sources]
+                    for slot in slots:
+                        wait_recv(far_in.at[slot], far_recv.at[slot])
+                    gave = paired(plane, third) and (plane % 2 == 0) != (plane < 2)
+                    terms = [far_in[slot].astype(FULL) for slot in slots]
+                    if not gave:
+                        terms.append(grad[dp, 2 * third + way].astype(FULL))
+                    total[2 * third + way] = sum(terms[1:], terms[0])
 
     steps = {
         "pair": pair_step,
@@ -584,6 +645,7 @@
         "first": first_step,
         "second": second_step,
         "third": third_step,
+        "chain": chain_step,
         "finish": finish_step,
     }
 
@@ -598,23 +660,29 @@
     core_copies[3].wait_recv()
     core_copies[4].wait_recv()
 
-    def reduce_rows(at):
-        cols = pl.ds(aligned(at * WIDTH, WIDTH), WIDTH)
-        part = dot_tn(
-            both(act_own[:, cols], act_oth[:, cols]), both(gred_own[:, own_384], gred_oth[...])
-        )
-        for unit in range(8):
+    reduced_both = both(gred_own[:, own_384], gred_oth[...])
+
+    def reduce_rows(first, count, before=0):
+        cols = slice(96 * (first - 64) - before, 96 * (first - 64 + count))
+        part = dot_tn(both(act_own[:, cols], act_oth[:, cols]), reduced_both)
+        for unit in range(count):
             for tile in range(3):
-                put_unit(64 + 8 * at + unit, slice(96 * tile, 96 * tile + 96), part[
-                    96 * unit : 96 * unit + 96, LANES * tile : LANES * tile + LANES
-                ])
-
-    @pl.loop(1, 4)
-    def _(at):
-        reduce_rows(at)
-
-    serve("reduce")
-    reduce_rows(0)
+                put_unit(
+                    first + unit,
+                    slice(96 * tile, 96 * tile + 96),
+                    part[
+                        before + 96 * unit : before + 96 * unit + 96,
+                        LANES * tile : LANES * tile + LANES,
+                    ],
+                )
+
+    for third in range(3):
+        for chip in range(12, CHIPS):
+            first = 6 * chip + 2 * third
+            reduce_rows(first, 2, before=96 * (first - 64) % LANES)
+        serve("reduce" + str(third))
+    reduce_rows(64, 8)
+    serve("reduce3")
 
     @pl.loop(0, 6)
     def _(at):
@@ -897,12 +965,12 @@
         wait_send(total.at[pl.ds(4, 2)], core_send.at[11])
 
     for plane in range(4):
-
-        @pl.when(jnp.logical_not(kept(plane)))
-        def _():
-            pair_copy(plane).wait_send()
-
         for third in range(3):
+            if paired(plane, third):
+
+                @pl.when(jnp.logical_not(kept(plane)))
+                def _():
+                    pair_copy(plane, third).wait_send()
 
             def sent():
                 for copy in first_copies(plane, third) + second_copies(plane, third):
@@ -910,7 +978,8 @@
 
                 @pl.when(zz != plane)
                 def _():
-                    far_copy(plane, third).wait_send()
+                    for way in range(2):
+                        far_copy(plane, third, way).wait_send()
 
             taking_part(plane, third, sent)
 
@@ -1030,28 +1099,28 @@
         low(BLOCK, WIDTH),
         low(BLOCK, WIDTH),
         low(CHIPS, 6, UNIT, LANES),
-        low(2, 4, 2, UNIT, LANES),
+        low(2, max(PAIRED), 4, 2, UNIT, LANES),
         low(4, 3, 4, UNIT, LANES),
         low(4, 3, 2, UNIT, LANES),
-        low(7, 2, UNIT, LANES),
+        low(18 + 6 * sum(CHAINED), UNIT, LANES),
         full(6, UNIT, LANES),
         full(3, UNIT, LANES),
         full(1816, LANES),
         full(1736, LANES),
         full(72, LANES),
         full(6, 72, LANES),
-        dma((7,)),
+        dma((9,)),
         dma((len(vectors),)),
         dma((12,)),
         dma((12,)),
-        dma((4,)),
-        dma((4,)),
+        dma((4, 3)),
+        dma((4, 3)),
         dma((4, 3, 4)),
         dma((4, 3, 4)),
         dma((4, 3, 2)),
         dma((4, 3, 2)),
-        dma((4, 3)),
-        dma((7,)),
+        dma((4, 3, 2)),
+        dma((18 + 6 * sum(CHAINED),)),
         dma((1,)),
         dma((6,)),
         dma((1,)),

time: 110 us -> 93.3 us (0.85)
  the two profiles are of different devices: /device:TPU:17 before, /device:TPU:1 now
where the time goes in v3:
time: 93.3 us; the launch traced here: 91.4 us
  Pallas kernels  88 us (94%)
  between operations  3.39 us (4%)
    pallas_call x1, Pallas kernels, fused_layer(): pl.pallas_call(layer_kernel, out_shape=results, in_specs=[anywhere] * 7 +...  85.6 us
    pallas_call x1, Pallas kernels, fused_layer(): pl.pallas_call(hand_over, out_shape=results, in_specs=[anywhere] * 3, out...  2.38 us

profile of v3, /device:TPU:1, one launch (start us, length us, event | category | flops | bytes accessed | tf_op | source)
XLA Modules:
  0.0 91.4 jit_solution(2877421773032925986)
XLA Ops:
  3.2 85.6 %encoder_layer.1 = (bf16[256,768]{1,0:T(8,128)(2,1)}, bf16[256,768]{1,0:T(8,128)(2,1)}, f32[1736,128]{1,0:T(8,128)}) custom-call(bf16[256,768]{1,0:T(8,128)(2,1)} %bitcast.8, bf16[256,768]{1,0:T(8,128)(2,1)} %bitcast.9, bf16[12,256,512]{2,1,0:T(8,128)(2,1)} %bitcast.7, bf16[768,2304]{1,0:T(8,128)(2,1)} %w_project.1, bf16[768,768]{1,0:T(8,128)(2,1)} %w_output.1, ...), custom_call_target="tpu_custom_call" | custom-call | tf_op jit(solution)/shard_map/encoder_layer/pallas_call | solution.py:1135
  88.9 2.4 %hand_over.1 = (bf16[256,768]{1,0:T(8,128)(2,1)}, bf16[256,768]{1,0:T(8,128)(2,1)}, f32[1736,128]{1,0:T(8,128)}) custom-call(bf16[256,768]{1,0:T(8,128)(2,1)} %get-tuple-element.9.refs_0_, bf16[256,768]{1,0:T(8,128)(2,1)} %get-tuple-element.10.refs_1_, f32[1736,128]{1,0:T(8,128)} %get-tuple-element.11.refs_2_), custom_call_target="tpu_custom_call" | custom-call | tf_op jit(solution)/shard_map/hand_over/pallas_call | solution.py:1156

commit v4 on v3

--- a/solution.py
+++ b/solution.py
@@ -48,91 +48,131 @@
 
 SCHEDULE = {
     "reduce0": (
+        ("first", 3, 1),
         ("first", 3, 0),
     ),
     "reduce1": (
-        ("first", 3, 1),
+        ("first", 3, 2),
     ),
     "reduce2": (
-        ("pair", 3, 2),
-    ),
-    "slopes": (
-        ("second", 3, 0),
+        ("first", 3, 3),
+        ("pair", 3, 4),
     ),
     "norm": (
+        ("second", 3, 0),
         ("second", 3, 1),
     ),
+    "expand": (
+        ("first", 2, 3),
+        ("first", 2, 2),
+        ("pair", 3, 5),
+    ),
     "output": (
-        ("pair", 1, 2),
+        ("pair", 1, 4),
         ("first", 1, 1),
+        ("first", 1, 0),
+        ("first", 2, 1),
+        ("first", 2, 0),
     ),
     "heads0": (
-        ("first", 1, 0),
+        ("third", 3, 0),
     ),
     "heads1": (
-        ("third", 3, 1),
-        ("second", 1, 1),
-        ("first", 2, 1),
-    ),
-    "heads2": (
-        ("third", 3, 0),
-        ("pair", 2, 2),
+        ("second", 3, 3),
+        ("first", 1, 3),
+        ("pair", 1, 5),
+        ("second", 2, 3),
+        ("pair", 2, 5),
     ),
     "keys": (
-        ("second", 1, 0),
+        ("second", 2, 2),
+        ("add", 3, 4),
+        ("add", 1, 4),
     ),
     "project": (
+        ("pair", 0, 5),
         ("first", 0, 0),
+        ("second", 1, 1),
+        ("first", 0, 3),
+        ("second", 1, 3),
+        ("second", 1, 0),
+        ("pair", 2, 4),
+        ("second", 1, 4),
+        ("first", 0, 4),
+        ("second", 2, 0),
         ("first", 0, 1),
+        ("third", 2, 3),
+        ("third", 2, 2),
+        ("bias", 0, 0),
     ),
     "input": (
+        ("third", 1, 1),
+        ("third", 3, 1),
+        ("second", 0, 3),
+        ("first", 0, 2),
+        ("second", 0, 4),
+        ("third", 1, 0),
         ("second", 0, 0),
     ),
-    "bias0": (
-        ("first", 0, 2),
-        ("chain", 3, 1),
+    "end": (
+        ("third", 1, 3),
+        ("bias", 1, 0),
+        ("third", 2, 0),
+        ("second", 3, 4),
+        ("third", 3, 3),
         ("second", 0, 1),
-        ("third", 1, 1),
-        ("add", 3, 2),
+        ("add", 2, 4),
         ("second", 2, 1),
-        ("chain", 3, 0),
+        ("third", 0, 3),
+        ("second", 0, 2),
+        ("third", 1, 4),
+        ("third", 0, 4),
+        ("add", 3, 5),
+        ("third", 3, 4),
+        ("second", 3, 2),
+        ("first", 1, 2),
+        ("add", 1, 5),
         ("third", 0, 0),
-        ("third", 1, 0),
-    ),
-    "bias1": (
-        ("second", 0, 2),
-        ("second", 3, 2),
-        ("first", 2, 0),
-    ),
-    "bias2": (
-        ("add", 1, 2),
         ("third", 0, 1),
-        ("add", 2, 2),
+        ("second", 2, 4),
+        ("add", 2, 5),
+        ("chain", 0, 3),
+        ("add", 0, 5),
+        ("bias", 2, 0),
+        ("chain", 0, 4),
+        ("third", 0, 2),
         ("third", 2, 1),
-        ("third", 0, 2),
+        ("third", 2, 4),
+        ("second", 1, 2),
+        ("second", 3, 5),
+        ("second", 2, 5),
+        ("chain", 0, 0),
+        ("chain", 0, 1),
         ("third", 3, 2),
-        ("chain", 0, 0),
-    ),
-    "bias3": (
-        ("second", 2, 0),
-        ("second", 1, 2),
-        ("second", 2, 2),
-        ("chain", 0, 1),
-        ("third", 2, 0),
+        ("second", 1, 5),
         ("chain", 0, 2),
         ("third", 1, 2),
-        ("third", 2, 2),
-    ),
-    "end0": (
+        ("third", 3, 5),
+        ("second", 0, 5),
+        ("third", 1, 5),
+        ("third", 0, 5),
         ("finish", 0, 0),
+        ("place", 0, 0),
+        ("finish", 0, 4),
         ("finish", 0, 1),
-    ),
-    "end1": (
+        ("third", 2, 5),
+        ("finish", 0, 3),
+        ("place", 0, 3),
+        ("place", 0, 4),
+        ("place", 0, 1),
         ("finish", 0, 2),
+        ("place", 0, 2),
+        ("finish", 0, 5),
+        ("place", 0, 5),
     ),
 }
-PAIRED = (0, 1, 1, 1)
-CHAINED = (True, False, False, True)
+PAIRED = (1, 2, 2, 2)
+CHAINED = (True, False, False, False)
 
 
 def aligned(start, step):
@@ -196,7 +236,6 @@
     second_in,
     far_in,
     total,
-    total_oth,
     flat,
     placed,
     bias_sum,
@@ -213,6 +252,7 @@
     second_recv,
     far_send,
     far_recv,
+    beside_send,
     bias_send,
     bias_recv,
     fix_send,
@@ -273,6 +313,7 @@
     greet(y_dev)
     for step in range(1, 4):
         greet((lax.rem(dp + 4 * step, CHIPS), blk))
+        greet((lax.rem(dp + 4 * step, CHIPS), oth))
 
     @pl.when((blk == 1) & (dp < CHIPS - 1))
     def _():
@@ -290,9 +331,8 @@
         copy.start()
         return copy
 
-    load_x.wait()
-    pl.semaphore_wait(barrier, 6 + ((blk == 0) & (dp > 0)).astype(jnp.int32))
-    core_copies = [to_core(0, x_row.at[own_rows], x_row.at[own_rows])]
+    pl.semaphore_wait(barrier, 9 + ((blk == 0) & (dp > 0)).astype(jnp.int32))
+    core_copies = [to_core(0, hidden, x_row.at[own_rows])]
 
     length, start_at, end_at, answered = (ref[...].reshape(1, 1) for ref in scalars)
     key_at = lax.broadcasted_iota(jnp.int32, (1, ROW), 1)
@@ -304,6 +344,7 @@
     def project(rows, part):
         return dot_nn(x_row[rows, :], wp[:, WIDTH * part : WIDTH * part + WIDTH])
 
+    load_x.wait()
     load_wp[0].wait()
     for copy in small:
         copy.wait()
@@ -335,16 +376,11 @@
     def pair_cols(head):
         return slice(LANES * (head // 2), LANES * (head // 2) + LANES)
 
-    def head_scores(head):
+    def score_part(head, part):
         cols = pair_cols(head)
-        scores = dot_nt(q_own[:, cols] * head_lanes[head % 2], k_row[:, cols])
-        return jnp.where(key_live, scores, -1e30)
-
-    def head_soft(scores):
-        peak = jnp.max(scores, axis=-1, keepdims=True)
-        terms = jnp.exp(scores - peak)
-        scale = 1.0 / jnp.sum(terms, axis=-1, keepdims=True)
-        return (terms * scale).astype(LOW)
+        keys = slice(BLOCK * part, BLOCK * part + BLOCK)
+        scores = dot_nt(q_own[:, cols] * head_lanes[head % 2], k_row[keys, cols])
+        return jnp.where(key_live[:, keys], scores, -1e30)
 
     gathered = {}
 
@@ -354,14 +390,28 @@
         if head % 2 == 1:
             att_own[:, cols] = (gathered[head - 1] + gathered[head]).astype(LOW)
 
-    ahead = head_scores(0)
+    def peak_of(part):
+        return jnp.max(part, axis=-1, keepdims=True)
+
+    def total_of(part):
+        return jnp.sum(part, axis=-1, keepdims=True)
+
+    ahead = [score_part(0, 0), score_part(0, 1)]
     for head in range(HEADS):
         scores = ahead
+        ahead = []
         if head + 1 < HEADS:
-            ahead = head_scores(head + 1)
+            ahead.append(score_part(head + 1, 0))
+        peak = jnp.maximum(peak_of(scores[0]), peak_of(scores[1]))
+        if head + 1 < HEADS:
+            ahead.append(score_part(head + 1, 1))
+        terms = [jnp.exp(part - peak) for part in scores]
         if head > 0:
             head_gather(head - 1)
-        soft[head] = head_soft(scores)
+        scale = 1.0 / (total_of(terms[0]) + total_of(terms[1]))
+        for part in range(2):
+            keys = slice(BLOCK * part, BLOCK * part + BLOCK)
+            soft[head, :, keys] = (terms[part] * scale).astype(LOW)
     head_gather(HEADS - 1)
     core_copies.append(to_core(1, att_own, att_oth))
 
@@ -377,16 +427,20 @@
 
     load_we.wait()
 
-    @pl.loop(0, 6, unroll=6)
-    def _(at):
-        cols = pl.ds(aligned(at * 512, 512), 512)
+    act_copies = []
+    for at in range(6):
+        cols = slice(512 * at, 512 * at + 512)
         expanded = dot_nn(mix_own[...], we[:, cols]) + expand_bias[:, cols]
         gate = 0.5 + 0.5 * lax.erf(expanded * (2.0**-0.5))
         bell = jnp.exp(expanded * expanded * -0.5) * ((2.0 * jnp.pi) ** -0.5)
         act_own[:, cols] = (expanded * gate).astype(LOW)
         slope[:, cols] = (gate + expanded * bell).astype(LOW)
-
-    core_copies.append(to_core(3, act_own, act_oth))
+        if at % 2 == 1:
+            piece = slice(512 * at - 512, 512 * at + 512)
+            act_copies.append(
+                to_core(9 + at // 2, act_own.at[:, piece], act_oth.at[:, piece])
+            )
+
     load_wr.wait()
     reduced = dot_nn(act_own[...], wr[...]) + reduce_bias[...]
     mixed = norm_one[...] * first_gain[...] + first_shift[...]
@@ -422,6 +476,7 @@
     put_bias(54, col_sum(pulled_low.astype(FULL)))
     own_384 = pl.ds(aligned(blk * 384, 384), 384)
     oth_384 = pl.ds(aligned(oth * 384, 384), 384)
+    core_copies.append(act_copies[0])
     core_copies.append(to_core(4, gred_own.at[:, oth_384], gred_oth))
 
     def send(src, dst, send_sem, recv_sem, dev):
@@ -463,163 +518,164 @@
             value = value + arrival.astype(FULL)
         grad[chip, unit] = value.astype(LOW)
 
-    def paired(plane, third):
-        return third >= 3 - PAIRED[plane]
+    def paired(plane, unit):
+        return unit >= 6 - PAIRED[plane]
 
     def kept(plane):
         return (lax.rem(zz, 2) == 0) if plane < 2 else (lax.rem(zz, 2) == 1)
 
-    def taking_part(plane, third, step):
-        if paired(plane, third):
+    def taking_part(plane, unit, step):
+        if paired(plane, unit):
             pl.when(kept(plane))(step)
         else:
             step()
 
-    def pair_copy(plane, third):
+    def pair_copy(plane, unit):
         return pltpu.make_async_remote_copy(
-            src_ref=grad.at[pl.ds(4 * plane, 4), pl.ds(2 * third, 2)],
-            dst_ref=pair_in.at[plane % 2, 2 - third],
-            send_sem=pair_send.at[plane, third],
-            recv_sem=pair_recv.at[plane, third],
+            src_ref=grad.at[pl.ds(4 * plane, 4), unit],
+            dst_ref=pair_in.at[plane % 2, 5 - unit],
+            send_sem=pair_send.at[plane, unit],
+            recv_sem=pair_recv.at[plane, unit],
             device_id=pair_dev,
             device_id_type=MESH,
         )
 
-    def first_copies(plane, third, slots=range(4)):
-        one, two = 2 * third, 2 * third + 1
+    def crossing(plane, unit):
+        x_first = (plane + unit) % 2 == 0
+        first_dev, second_dev = (x_dev, y_dev) if x_first else (y_dev, x_dev)
+        beside = owner(plane, 1 - xx, yy) if x_first else owner(plane, xx, 1 - yy)
+        behind = owner(plane, xx, 1 - yy) if x_first else owner(plane, 1 - xx, yy)
+        return first_dev, second_dev, beside, behind
+
+    def first_copies(plane, unit, slots=(0, 1)):
+        first_dev, _, beside, _ = crossing(plane, unit)
+        chips = (owner(plane, 1 - xx, 1 - yy), beside)
         return [
             pltpu.make_async_remote_copy(
-                src_ref=grad.at[chip, unit],
-                dst_ref=first_in.at[plane, third, slot],
-                send_sem=first_send.at[plane, third, slot],
-                recv_sem=first_recv.at[plane, third, slot],
-                device_id=dev,
+                src_ref=grad.at[chips[slot], unit],
+                dst_ref=first_in.at[plane, unit, slot],
+                send_sem=first_send.at[plane, unit, slot],
+                recv_sem=first_recv.at[plane, unit, slot],
+                device_id=first_dev,
                 device_id_type=MESH,
             )
-            for chip, unit, slot, dev in (
-                (owner(plane, 1 - xx, 1 - yy), one, 0, x_dev),
-                (owner(plane, 1 - xx, 1 - yy), two, 1, y_dev),
-                (owner(plane, 1 - xx, yy), one, 2, x_dev),
-                (owner(plane, xx, 1 - yy), two, 3, y_dev),
-            )
-            if slot in slots
+            for slot in slots
         ]
 
-    def second_copies(plane, third):
-        one, two = 2 * third, 2 * third + 1
-        return [
-            pltpu.make_async_remote_copy(
-                src_ref=grad.at[chip, unit],
-                dst_ref=second_in.at[plane, third, slot],
-                send_sem=second_send.at[plane, third, slot],
-                recv_sem=second_recv.at[plane, third, slot],
-                device_id=dev,
-                device_id_type=MESH,
-            )
-            for chip, unit, slot, dev in (
-                (owner(plane, xx, 1 - yy), one, 0, y_dev),
-                (owner(plane, 1 - xx, yy), two, 1, x_dev),
-            )
-        ]
-
-    def chained(plane, third):
-        return CHAINED[plane] and not paired(plane, third)
-
-    def last_slot(third, source, way):
-        return 6 * third + 2 * source + way
-
-    def passing_slot(plane, third, way):
-        return 18 + 6 * sum(CHAINED[:plane]) + 2 * third + way
-
-    def far_copy(plane, third, way):
-        below = zz < plane
-        if chained(plane, third):
-            target = jnp.where(below, dp + 4, dp - 4)
-            ends = jnp.where(below, zz + 1, zz - 1) == plane
-            passing = passing_slot(plane, third, way)
-            slot = jnp.where(ends, last_slot(third, jnp.where(below, 0, 1), way), passing)
-        else:
-            target = owner(plane, xx, yy)
-            slot = last_slot(third, jnp.where(below, zz, zz - 1), way)
+    def second_copy(plane, unit):
+        _, second_dev, _, behind = crossing(plane, unit)
         return pltpu.make_async_remote_copy(
-            src_ref=grad.at[owner(plane, xx, yy), 2 * third + way],
-            dst_ref=far_in.at[slot],
-            send_sem=far_send.at[plane, third, way],
-            recv_sem=far_recv.at[slot],
-            device_id=(target, blk),
+            src_ref=grad.at[behind, unit],
+            dst_ref=second_in.at[plane, unit],
+            send_sem=second_send.at[plane, unit],
+            recv_sem=second_recv.at[plane, unit],
+            device_id=second_dev,
             device_id_type=MESH,
         )
 
-    def pair_step(plane, third):
+    def chained(plane, unit):
+        return CHAINED[plane] and not paired(plane, unit)
+
+    def last_slot(unit, source):
+        return jnp.where(blk == unit // 3, 0, 12) + 4 * (unit % 3) + source
+
+    def passing_slot(plane, unit):
+        return 24 + 6 * sum(CHAINED[:plane]) + unit
+
+    def far_copy(plane, unit):
+        below = zz < plane
+        core = unit // 3
+        if chained(plane, unit):
+            chip = jnp.where(below, dp + 4, dp - 4)
+            ends = jnp.where(below, zz + 1, zz - 1) == plane
+            last = last_slot(unit, jnp.where(below, 0, 1))
+            slot = jnp.where(ends, last, passing_slot(plane, unit))
+            core = jnp.where(ends, core, blk)
+        else:
+            chip = owner(plane, xx, yy)
+            slot = last_slot(unit, jnp.where(below, zz, zz - 1))
+        return pltpu.make_async_remote_copy(
+            src_ref=grad.at[owner(plane, xx, yy), unit],
+            dst_ref=far_in.at[slot],
+            send_sem=far_send.at[plane, unit],
+            recv_sem=far_recv.at[slot],
+            device_id=(chip, core),
+            device_id_type=MESH,
+        )
+
+    def beside_copy(unit):
+        slot = 12 + 4 * (unit % 3) + 3
+        return pltpu.make_async_remote_copy(
+            src_ref=grad.at[dp, unit],
+            dst_ref=far_in.at[slot],
+            send_sem=beside_send.at[unit % 3],
+            recv_sem=far_recv.at[slot],
+            device_id=core_dev,
+            device_id_type=MESH,
+        )
+
+    def pair_step(plane, unit):
         @pl.when(jnp.logical_not(kept(plane)))
         def _():
-            pair_copy(plane, third).start()
-
-    def pair_add(plane, third):
+            pair_copy(plane, unit).start()
+
+    def pair_add(plane, unit):
         @pl.when(kept(plane))
         def _():
-            pair_copy(plane, third).wait_recv()
+            pair_copy(plane, unit).wait_recv()
 
             @pl.loop(0, 4)
             def _(chip):
-                for way in range(2):
-                    add_unit(
-                        4 * plane + chip,
-                        2 * third + way,
-                        [pair_in[plane % 2, 2 - third, chip, way]],
-                    )
-
-            for copy in first_copies(plane, third):
+                add_unit(4 * plane + chip, unit, [pair_in[plane % 2, 5 - unit, chip]])
+
+            for copy in first_copies(plane, unit):
                 copy.start()
 
-    def first_step(plane, third):
-        for copy in first_copies(plane, third):
+    def first_step(plane, unit):
+        for copy in first_copies(plane, unit):
             copy.start()
 
-    def second_step(plane, third):
+    def second_step(plane, unit):
         def step():
-            firsts = first_copies(plane, third, (0, 1))
-            seconds = second_copies(plane, third)
-            for way in range(2):
-                chip = (owner(plane, xx, 1 - yy), owner(plane, 1 - xx, yy))[way]
-                firsts[way].wait_recv()
-                add_unit(chip, 2 * third + way, [first_in[plane, third, way]])
-                seconds[way].start()
-
-        taking_part(plane, third, step)
-
-    def third_step(plane, third):
+            first_copies(plane, unit, (0,))[0].wait_recv()
+            _, _, _, behind = crossing(plane, unit)
+            add_unit(behind, unit, [first_in[plane, unit, 0]])
+            second_copy(plane, unit).start()
+
+        taking_part(plane, unit, step)
+
+    def third_step(plane, unit):
         def step():
-            firsts = first_copies(plane, third, (2, 3))
-            seconds = second_copies(plane, third)
-            for way in range(2):
-                firsts[way].wait_recv()
-                seconds[way].wait_recv()
-                add_unit(
-                    owner(plane, xx, yy),
-                    2 * third + way,
-                    [first_in[plane, third, 2 + way], second_in[plane, third, way]],
-                )
-                leaves = (zz == 0) | (zz == 3) if chained(plane, third) else zz >= 0
-
-                @pl.when((zz != plane) & leaves)
-                def _():
-                    far_copy(plane, third, way).start()
-
-        taking_part(plane, third, step)
-
-    def chain_step(plane, third):
+            first_copies(plane, unit, (1,))[0].wait_recv()
+            second_copy(plane, unit).wait_recv()
+            add_unit(
+                owner(plane, xx, yy), unit, [first_in[plane, unit, 1], second_in[plane, unit]]
+            )
+            leaves = zz != plane
+            if chained(plane, unit):
+                leaves = leaves & ((zz == 0) | (zz == 3))
+
+            @pl.when(leaves)
+            def _():
+                far_copy(plane, unit).start()
+
+            @pl.when((zz == plane) & (blk != unit // 3))
+            def _():
+                beside_copy(unit).start()
+
+        taking_part(plane, unit, step)
+
+    def chain_step(plane, unit):
         @pl.when((zz != plane) & (zz > 0) & (zz < 3))
         def _():
-            for way in range(2):
-                slot = passing_slot(plane, third, way)
-                wait_recv(far_in.at[slot], far_recv.at[slot])
-                add_unit(owner(plane, xx, yy), 2 * third + way, [far_in[slot]])
-                far_copy(plane, third, way).start()
-
-    def finish_step(_, third):
+            slot = passing_slot(plane, unit)
+            wait_recv(far_in.at[slot], far_recv.at[slot])
+            add_unit(owner(plane, xx, yy), unit, [far_in[slot]])
+            far_copy(plane, unit).start()
+
+    def finish_step(_, unit):
         for plane in range(4):
-            if paired(plane, third):
+            if paired(plane, unit):
                 sources = [z for z in range(4) if z != plane and (z % 2 == 0) == (plane < 2)]
                 sources = [z if z < plane else z - 1 for z in sources]
             elif CHAINED[plane]:
@@ -627,19 +683,100 @@
             else:
                 sources = [0, 1, 2]
 
-            @pl.when(zz == plane)
+            gave = paired(plane, unit) and (plane % 2 == 0) != (plane < 2)
+
+            @pl.when((zz == plane) & (blk == unit // 3))
             def _():
-                for way in range(2):
-                    slots = [last_slot(third, source, way) for source in sources]
+                for half in range(2):
+                    first = 12 * half + 4 * (unit % 3)
+                    slots = [first + source for source in sources]
+                    if half == 1 and not gave:
+                        slots.append(first + 3)
                     for slot in slots:
                         wait_recv(far_in.at[slot], far_recv.at[slot])
-                    gave = paired(plane, third) and (plane % 2 == 0) != (plane < 2)
                     terms = [far_in[slot].astype(FULL) for slot in slots]
-                    if not gave:
-                        terms.append(grad[dp, 2 * third + way].astype(FULL))
-                    total[2 * third + way] = sum(terms[1:], terms[0])
+                    if half == 0 and not gave:
+                        terms.append(grad[dp, unit].astype(FULL))
+                    total[half, unit % 3] = sum(terms[1:], terms[0])
+
+    def place_step(_, unit):
+        core, local = unit // 3, unit % 3
+
+        @pl.when(blk == core)
+        def _():
+            lay_out(0, core, local)
+            lay_out(1, 1 - core, local)
+            if unit == 0:
+                @pl.when(dp > 0)
+                def _():
+                    hand_back((dp - 1, 1))
+
+            elif unit == 3:
+                hand_back(core_dev)
+            if local < 2:
+                move_rows(*((0, 9), (9, 19))[local])
+
+    def lay_out(half, column_half, local):
+        kind_at = 3 * device + local
+        kinds = (
+            (kind_at < 24, 32, 9),
+            (((kind_at >= 24) & (kind_at < 32)) | (kind_at >= 64), 96, 3),
+            ((kind_at >= 32) & (kind_at < 64), 24, 12),
+        )
+        for fits, rows, tiles in kinds:
+
+            @pl.when(fits)
+            def _():
+                for tile in range(tiles):
+                    for group in range(rows // 8):
+                        at = rows * tile + 8 * group
+                        to = 576 * local + 16 * group * tiles + tile + column_half * tiles
+                        flat[pl.ds(to, 8, stride=2 * tiles), :] = total[
+                            half, local, at : at + 8, :
+                        ]
+
+    def hand_back(dev):
+        send(flat.at[0:72], flat.at[1728:1800], fix_send.at[0], fix_recv.at[0], dev)
+
+    shift = 32 * lax.rem(device, 4)
+    skip = (9 * device) // 4
+    stays = lane < LANES - shift
+
+    def move_rows(first, last):
+        @pl.loop(first, last)
+        def _(at):
+            rows = at * 56
+            one = pltpu.roll(flat[pl.ds(rows + skip, 56), :], LANES - shift, 1)
+            two = pltpu.roll(flat[pl.ds(rows + skip + 1, 56), :], LANES - shift, 1)
+            placed[pl.ds(aligned(rows, 8), 56), :] = jnp.where(stays, one, two)
+
+    corner = (xx == 1) & (yy == 1)
+    last = dp == CHIPS - 1
+
+    def bias_step(hop, _):
+        def leaves(here, slot, dev):
+            @pl.when(here)
+            def _():
+                send(bias_sum, bias_in.at[slot], bias_send.at[0], bias_recv.at[slot], dev)
+
+        def comes(here, slot):
+            @pl.when(here)
+            def _():
+                wait_recv(bias_in.at[slot], bias_recv.at[slot])
+                bias_sum[...] += bias_in[slot]
+
+        if hop == 0:
+            leaves(xx == 0, 0, x_dev)
+        elif hop == 1:
+            comes(xx == 1, 0)
+            leaves((xx == 1) & (yy == 0), 1, y_dev)
+        else:
+            comes(corner, 1)
+            leaves(corner & (zz < 3), 2 + 2 * zz + blk, (CHIPS - 1, 1))
+            leaves(last & (blk == 0), 8, core_dev)
 
     steps = {
+        "bias": bias_step,
         "pair": pair_step,
         "add": pair_add,
         "first": first_step,
@@ -647,17 +784,19 @@
         "third": third_step,
         "chain": chain_step,
         "finish": finish_step,
+        "place": place_step,
     }
 
     def serve(after):
-        for what, plane, third in SCHEDULE.get(after, ()):
-            steps[what](plane, third)
+        for what, plane, unit in SCHEDULE.get(after, ()):
+            steps[what](plane, unit)
 
     def put_unit(at, rows, values):
         chip, unit = (at // 6, at % 6) if isinstance(at, int) else (lax.div(at, 6), lax.rem(at, 6))
         grad[chip, unit, rows, :] = values.astype(LOW)
 
-    core_copies[3].wait_recv()
+    for copy in act_copies:
+        copy.wait_recv()
     core_copies[4].wait_recv()
 
     reduced_both = both(gred_own[:, own_384], gred_oth[...])
@@ -684,21 +823,21 @@
     reduce_rows(64, 8)
     serve("reduce3")
 
-    @pl.loop(0, 6)
-    def _(at):
-        half = jnp.where(at < 3, oth, blk)
-        part_at = lax.rem(at, 3) * 512
+    for at in range(6):
+        half = oth if at < 3 else blk
+        part_at = at % 3 * 512
         cols = pl.ds(aligned(half * 1536 + part_at, 512), 512)
         grad_active = dot_nt(gred_own[...], wr[cols, :])
         grad_expanded = (grad_active * slope[:, cols].astype(FULL)).astype(LOW)
-        gexp_own[half, :, pl.ds(aligned(part_at, 512), 512)] = grad_expanded
+        gexp_own[half, :, part_at : part_at + 512] = grad_expanded
         sums = col_sum(grad_expanded.astype(FULL))
         for tile in range(4):
-            bias_sum[pl.ds(30 + half * 12 + lax.rem(at, 3) * 4 + tile, 1), :] = sums[
+            bias_sum[pl.ds(30 + half * 12 + at % 3 * 4 + tile, 1), :] = sums[
                 :, LANES * tile : LANES * tile + LANES
             ]
-
-    core_copies.append(to_core(5, gexp_own.at[oth], gexp_oth))
+        if at == 2:
+            core_copies.append(to_core(5, gexp_own.at[oth], gexp_oth))
+
     serve("slopes")
     grad_mixed = resid_two[...]
     for half in range(2):
@@ -722,7 +861,7 @@
     core_copies[2].wait_recv()
     core_copies[5].wait_recv()
 
-    @pl.loop(0, 6)
+    @pl.loop(0, 6, unroll=3)
     def _(at):
         cols = pl.ds(aligned(at * 256, 256), 256)
         part = dot_tn(
@@ -809,7 +948,7 @@
 
     core_copies[8].wait_recv()
 
-    @pl.loop(0, 3)
+    @pl.loop(0, 3, unroll=3)
     def _(at):
         cols = pl.ds(aligned(at * 384, 384), 384)
         mine = pl.ds(aligned(blk * 1152 + at * 384, 384), 384)
@@ -827,161 +966,53 @@
     input_gradient_part()
     serve("input")
 
-    def bias_leaves(at, here, dev):
-        @pl.when(here)
-        def _():
-            send(bias_sum, bias_in.at[at], bias_send.at[0], bias_recv.at[at], dev)
-
-    def bias_comes(at, there):
-        @pl.when(there)
-        def _():
-            wait_recv(bias_in.at[at], bias_recv.at[at])
-            bias_sum[...] += bias_in[at]
-
-    corner = (xx == 1) & (yy == 1)
-    last = dp == CHIPS - 1
-    bias_leaves(0, xx == 0, x_dev)
-    serve("bias0")
-    bias_comes(0, xx == 1)
-    bias_leaves(1, (xx == 1) & (yy == 0), y_dev)
-    serve("bias1")
-    bias_comes(1, corner)
-
-    @pl.when(corner & (zz < 3))
-    def _():
-        send(
-            bias_sum,
-            bias_in.at[2 + zz],
-            bias_send.at[0],
-            bias_recv.at[2 + zz],
-            (CHIPS - 1, blk),
-        )
-
-    serve("bias2")
-
-    @pl.when(last)
-    def _():
-        for at in range(2, 5):
-            wait_recv(bias_in.at[at], bias_recv.at[at])
-            bias_sum[...] += bias_in[at]
-
-    @pl.when(last & (blk == 0))
-    def _():
-        send(bias_sum, bias_in.at[5], bias_send.at[0], bias_recv.at[5], core_dev)
-
-    serve("bias3")
+    serve("end")
 
     @pl.when(last & (blk == 1))
     def _():
-        wait_recv(bias_in.at[5], bias_recv.at[5])
-        flat[1728:1800, :] = bias_sum[...] + bias_in[5]
-
-    def lay_out(source, first, column_half, unit):
-        kind_at = 3 * device + unit
-        kinds = (
-            (kind_at < 24, 32, 9),
-            (((kind_at >= 24) & (kind_at < 32)) | (kind_at >= 64), 96, 3),
-            ((kind_at >= 32) & (kind_at < 64), 24, 12),
-        )
-        for fits, rows, tiles in kinds:
-
-            @pl.when(fits)
-            def _():
-                for tile in range(tiles):
-                    for group in range(rows // 8):
-                        at = rows * tile + 8 * group
-                        to = 576 * unit + 16 * group * tiles + tile + column_half * tiles
-                        flat[pl.ds(to, 8, stride=2 * tiles), :] = source[
-                            first + unit, at : at + 8, :
-                        ]
-
-    def to_core_when(at, here, src, dst):
-        @pl.when(here)
-        def _():
-            send(src, dst, core_send.at[at], core_recv.at[at], core_dev)
-
-    serve("end0")
-    to_core_when(9, blk == 1, total.at[pl.ds(0, 3)], total_oth)
-    to_core_when(10, blk == 0, total.at[pl.ds(3, 1)], total_oth.at[pl.ds(0, 1)])
-
-    @pl.when(blk == 1)
-    def _():
-        lay_out(total, 3, 1, 0)
-        wait_recv(total_oth.at[pl.ds(0, 1)], core_recv.at[10])
-        lay_out(total_oth, 0, 0, 0)
-        send(flat.at[0:72], flat.at[1728:1800], fix_send.at[0], fix_recv.at[0], core_dev)
-
-    @pl.when(blk == 0)
-    def _():
-        for unit in range(3):
-            lay_out(total, 0, 0, unit)
-        wait_recv(total_oth, core_recv.at[9])
-        for unit in range(3):
-            lay_out(total_oth, 0, 1, unit)
-
-        @pl.when(dp > 0)
-        def _():
-            send(flat.at[0:72], flat.at[1728:1800], fix_send.at[0], fix_recv.at[0], (dp - 1, 1))
-
-    serve("end1")
-    to_core_when(11, blk == 0, total.at[pl.ds(4, 2)], total_oth.at[pl.ds(1, 2)])
-
-    @pl.when(blk == 1)
-    def _():
-        for unit in range(1, 3):
-            lay_out(total, 3, 1, unit)
-        wait_recv(total_oth.at[pl.ds(1, 2)], core_recv.at[11])
-        for unit in range(1, 3):
-            lay_out(total_oth, 0, 0, unit)
+        for at in range(2, 9):
+            wait_recv(bias_in.at[at], bias_recv.at[at])
+        flat[1728:1800, :] = sum((bias_in[at] for at in range(2, 9)), bias_sum[...])
 
     @pl.when(device < 2 * CHIPS - 1)
     def _():
         wait_recv(flat.at[1728:1800], fix_recv.at[0])
 
-    shift = 32 * lax.rem(device, 4)
-    skip = (9 * device) // 4
-    stays = lane < LANES - shift
-
-    @pl.loop(0, 31)
-    def _(at):
-        rows = at * 56
-        first = pltpu.roll(flat[pl.ds(rows + skip, 56), :], LANES - shift, 1)
-        second = pltpu.roll(flat[pl.ds(rows + skip + 1, 56), :], LANES - shift, 1)
-        placed[pl.ds(aligned(rows, 8), 56), :] = jnp.where(stays, first, second)
-
-    store_grads = pltpu.make_async_copy(placed, grads, out_sem.at[2])
-    store_grads.start()
-
-    for copy in core_copies:
+    early = pl.ds(0, 19 * 56)
+    late = pl.ds(19 * 56, 12 * 56)
+    stores = [
+        pltpu.make_async_copy(placed.at[rows], grads.at[rows], out_sem.at[2 + at])
+        for at, rows in enumerate((early, late))
+    ]
+    stores[0].start()
+    move_rows(19, 31)
+    stores[1].start()
+
+    for copy in core_copies + act_copies[1:]:
         copy.wait_send()
 
-    @pl.when(blk == 1)
-    def _():
-        wait_send(total.at[pl.ds(0, 3)], core_send.at[9])
-
-    @pl.when(blk == 0)
-    def _():
-        wait_send(total.at[pl.ds(3, 1)], core_send.at[10])
-        wait_send(total.at[pl.ds(4, 2)], core_send.at[11])
-
     for plane in range(4):
-        for third in range(3):
-            if paired(plane, third):
+        for unit in range(6):
+            if paired(plane, unit):
 
                 @pl.when(jnp.logical_not(kept(plane)))
                 def _():
-                    pair_copy(plane, third).wait_send()
+                    pair_copy(plane, unit).wait_send()
 
             def sent():
-                for copy in first_copies(plane, third) + second_copies(plane, third):
+                for copy in first_copies(plane, unit):
                     copy.wait_send()
+                second_copy(plane, unit).wait_send()
 
                 @pl.when(zz != plane)
                 def _():
-                    for way in range(2):
-                        far_copy(plane, third, way).wait_send()
-
-            taking_part(plane, third, sent)
+                    far_copy(plane, unit).wait_send()
+
+                @pl.when((zz == plane) & (blk != unit // 3))
+                def _():
+                    beside_copy(unit).wait_send()
+
+            taking_part(plane, unit, sent)
 
     @pl.when(jnp.logical_not(last & (blk == 1)))
     def _():
@@ -993,15 +1024,23 @@
 
     store_out.wait()
     pltpu.make_async_copy(gin_own, input_gradient, out_sem.at[1]).wait()
-    store_grads.wait()
+    for store in stores:
+        store.wait()
 
 
 def hand_over(*refs):
     sources, targets, held, sems = refs[:3], refs[3:6], refs[6:9], refs[9]
-    reads = [pltpu.make_async_copy(*pair, sems.at[at]) for at, pair in enumerate(zip(sources, held))]
-    writes = [
-        pltpu.make_async_copy(*pair, sems.at[3 + at]) for at, pair in enumerate(zip(held, targets))
-    ]
+    pieces = []
+    for source, target, buffer in zip(sources, targets, held):
+        rows = 248 if source.shape[0] % 248 == 0 else source.shape[0]
+        for first in range(0, source.shape[0], rows):
+            piece = pl.ds(first, rows)
+            pieces.append((source.at[piece], buffer.at[piece], target.at[piece]))
+    reads = []
+    writes = []
+    for at, (source, buffer, target) in enumerate(pieces):
+        reads.append(pltpu.make_async_copy(source, buffer, sems.at[0, at]))
+        writes.append(pltpu.make_async_copy(buffer, target, sems.at[1, at]))
     for read in reads:
         read.start()
     for read, write in zip(reads, writes):
@@ -1099,33 +1138,33 @@
         low(BLOCK, WIDTH),
         low(BLOCK, WIDTH),
         low(CHIPS, 6, UNIT, LANES),
-        low(2, max(PAIRED), 4, 2, UNIT, LANES),
-        low(4, 3, 4, UNIT, LANES),
-        low(4, 3, 2, UNIT, LANES),
-        low(18 + 6 * sum(CHAINED), UNIT, LANES),
-        full(6, UNIT, LANES),
-        full(3, UNIT, LANES),
+        low(2, max(PAIRED), 4, UNIT, LANES),
+        low(4, 6, 2, UNIT, LANES),
+        low(4, 6, UNIT, LANES),
+        low(24 + 6 * sum(CHAINED), UNIT, LANES),
+        full(2, 3, UNIT, LANES),
         full(1816, LANES),
         full(1736, LANES),
         full(72, LANES),
-        full(6, 72, LANES),
+        full(9, 72, LANES),
         dma((9,)),
         dma((len(vectors),)),
         dma((12,)),
         dma((12,)),
-        dma((4, 3)),
-        dma((4, 3)),
-        dma((4, 3, 4)),
-        dma((4, 3, 4)),
-        dma((4, 3, 2)),
-        dma((4, 3, 2)),
-        dma((4, 3, 2)),
-        dma((18 + 6 * sum(CHAINED),)),
+        dma((4, 6)),
+        dma((4, 6)),
+        dma((4, 6, 2)),
+        dma((4, 6, 2)),
+        dma((4, 6)),
+        dma((4, 6)),
+        dma((4, 6)),
+        dma((24 + 6 * sum(CHAINED),)),
+        dma((3,)),
         dma((1,)),
-        dma((6,)),
+        dma((9,)),
         dma((1,)),
         dma((1,)),
-        dma((3,)),
+        dma((4,)),
     ]
     results = (
         jax.ShapeDtypeStruct((BLOCK, WIDTH), LOW),
@@ -1158,7 +1197,7 @@
         out_shape=results,
         in_specs=[anywhere] * 3,
         out_specs=(anywhere,) * 3,
-        scratch_shapes=[pltpu.VMEM(result.shape, result.dtype) for result in results] + [dma((6,))],
+        scratch_shapes=[pltpu.VMEM(result.shape, result.dtype) for result in results] + [dma((2, 9))],
         name="hand_over",
     )(*made)
     return (

time: 93.3 us -> 86.8 us (0.930); the launches traced: 91.4 us -> 86.7 us
  Pallas kernels: 88 us -> 83.2 us
    pallas_call x1, Pallas kernels: 85.6 us -> 80.9 us  [fused_layer(): pl.pallas_call(layer_kernel, out_shape=results, in_specs=[anywhere] * 7 +...]
where the time goes in v4:
time: 86.8 us; the launch traced here: 86.7 us
  Pallas kernels  83.2 us (96%)
  between operations  3.41 us (4%)
    pallas_call x1, Pallas kernels, fused_layer(): pl.pallas_call(layer_kernel, out_shape=results, in_specs=[anywhere] * 7 +...  80.9 us
    pallas_call x1, Pallas kernels, fused_layer(): pl.pallas_call(hand_over, out_shape=results, in_specs=[anywhere] * 3, out...  2.31 us

profile of v4, /device:TPU:1, one launch (start us, length us, event | category | flops | bytes accessed | tf_op | source)
XLA Modules:
  0.0 86.7 jit_solution(14778666454228579454)
XLA Ops:
  3.2 80.9 %encoder_layer.1 = (bf16[256,768]{1,0:T(8,128)(2,1)}, bf16[256,768]{1,0:T(8,128)(2,1)}, f32[1736,128]{1,0:T(8,128)}) custom-call(bf16[256,768]{1,0:T(8,128)(2,1)} %bitcast.8, bf16[256,768]{1,0:T(8,128)(2,1)} %bitcast.9, bf16[12,256,512]{2,1,0:T(8,128)(2,1)} %bitcast.7, bf16[768,2304]{1,0:T(8,128)(2,1)} %w_project.1, bf16[768,768]{1,0:T(8,128)(2,1)} %w_output.1, ...), custom_call_target="tpu_custom_call" | custom-call | tf_op jit(solution)/shard_map/encoder_layer/pallas_call | solution.py:1174
  84.2 2.3 %hand_over.1 = (bf16[256,768]{1,0:T(8,128)(2,1)}, bf16[256,768]{1,0:T(8,128)(2,1)}, f32[1736,128]{1,0:T(8,128)}) custom-call(bf16[256,768]{1,0:T(8,128)(2,1)} %get-tuple-element.9.refs_0_, bf16[256,768]{1,0:T(8,128)(2,1)} %get-tuple-element.10.refs_1_, f32[1736,128]{1,0:T(8,128)} %get-tuple-element.11.refs_2_), custom_call_target="tpu_custom_call" | custom-call | tf_op jit(solution)/shard_map/hand_over/pallas_call | solution.py:1195

commit v5 on v4

--- a/solution.py
+++ b/solution.py
@@ -52,126 +52,124 @@
         ("first", 3, 0),
     ),
     "reduce1": (
-        ("first", 3, 2),
+        ("first", 3, 3),
     ),
     "reduce2": (
-        ("first", 3, 3),
-        ("pair", 3, 4),
+        ("first", 3, 4),
+        ("pair", 3, 5),
     ),
     "norm": (
+        ("pair", 3, 2),
         ("second", 3, 0),
         ("second", 3, 1),
     ),
     "expand": (
-        ("first", 2, 3),
-        ("first", 2, 2),
-        ("pair", 3, 5),
+        ("second", 3, 3),
+        ("first", 2, 4),
     ),
     "output": (
-        ("pair", 1, 4),
         ("first", 1, 1),
-        ("first", 1, 0),
+        ("pair", 1, 5),
         ("first", 2, 1),
-        ("first", 2, 0),
     ),
     "heads0": (
-        ("third", 3, 0),
+        ("first", 1, 0),
     ),
-    "heads1": (
-        ("second", 3, 3),
+    "heads4": (
+        ("second", 2, 1),
+        ("pair", 1, 2),
+        ("third", 3, 1),
+    ),
+    "heads5": (
+        ("second", 1, 1),
+        ("first", 2, 3),
+        ("second", 2, 4),
+        ("pair", 2, 2),
         ("first", 1, 3),
-        ("pair", 1, 5),
-        ("second", 2, 3),
-        ("pair", 2, 5),
-    ),
-    "keys": (
-        ("second", 2, 2),
-        ("add", 3, 4),
-        ("add", 1, 4),
+        ("first", 2, 0),
     ),
     "project": (
         ("pair", 0, 5),
+        ("third", 2, 1),
+        ("second", 1, 0),
+        ("second", 1, 3),
+        ("first", 0, 1),
+        ("first", 0, 4),
+        ("third", 1, 1),
+        ("second", 2, 0),
         ("first", 0, 0),
-        ("second", 1, 1),
-        ("first", 0, 3),
-        ("second", 1, 3),
-        ("second", 1, 0),
-        ("pair", 2, 4),
-        ("second", 1, 4),
-        ("first", 0, 4),
-        ("second", 2, 0),
-        ("first", 0, 1),
-        ("third", 2, 3),
-        ("third", 2, 2),
-        ("bias", 0, 0),
-    ),
-    "input": (
-        ("third", 1, 1),
-        ("third", 3, 1),
-        ("second", 0, 3),
-        ("first", 0, 2),
-        ("second", 0, 4),
-        ("third", 1, 0),
-        ("second", 0, 0),
+        ("third", 3, 0),
+        ("pair", 2, 5),
+        ("third", 2, 4),
     ),
     "end": (
+        ("first", 0, 3),
+        ("second", 0, 1),
         ("third", 1, 3),
+        ("first", 0, 2),
+        ("second", 0, 0),
+        ("second", 0, 4),
+        ("second", 0, 3),
+        ("third", 3, 3),
+        ("third", 1, 0),
+        ("third", 0, 1),
+        ("bias", 0, 0),
+        ("add", 2, 2),
+        ("second", 3, 4),
+        ("first", 1, 4),
+        ("second", 2, 3),
+        ("second", 0, 2),
+        ("third", 0, 0),
+        ("third", 0, 4),
+        ("third", 2, 0),
+        ("second", 1, 4),
+        ("add", 3, 5),
+        ("add", 2, 5),
+        ("second", 2, 2),
+        ("chain", 0, 1),
+        ("add", 0, 5),
+        ("add", 3, 2),
+        ("third", 0, 3),
+        ("add", 1, 5),
         ("bias", 1, 0),
-        ("third", 2, 0),
-        ("second", 3, 4),
-        ("third", 3, 3),
-        ("second", 0, 1),
-        ("add", 2, 4),
-        ("second", 2, 1),
-        ("third", 0, 3),
-        ("second", 0, 2),
+        ("chain", 0, 0),
+        ("third", 0, 2),
+        ("third", 3, 4),
+        ("chain", 0, 4),
+        ("add", 1, 2),
+        ("third", 2, 2),
+        ("third", 2, 3),
+        ("second", 2, 5),
+        ("second", 3, 5),
+        ("second", 3, 2),
         ("third", 1, 4),
-        ("third", 0, 4),
-        ("add", 3, 5),
-        ("third", 3, 4),
-        ("second", 3, 2),
-        ("first", 1, 2),
-        ("add", 1, 5),
-        ("third", 0, 0),
-        ("third", 0, 1),
-        ("second", 2, 4),
-        ("add", 2, 5),
+        ("second", 0, 5),
         ("chain", 0, 3),
-        ("add", 0, 5),
         ("bias", 2, 0),
-        ("chain", 0, 4),
-        ("third", 0, 2),
-        ("third", 2, 1),
-        ("third", 2, 4),
-        ("second", 1, 2),
-        ("second", 3, 5),
-        ("second", 2, 5),
-        ("chain", 0, 0),
-        ("chain", 0, 1),
-        ("third", 3, 2),
         ("second", 1, 5),
         ("chain", 0, 2),
+        ("third", 0, 5),
+        ("third", 2, 5),
+        ("finish", 0, 1),
+        ("second", 1, 2),
+        ("third", 3, 5),
+        ("third", 1, 5),
+        ("finish", 0, 0),
         ("third", 1, 2),
-        ("third", 3, 5),
-        ("second", 0, 5),
-        ("third", 1, 5),
-        ("third", 0, 5),
-        ("finish", 0, 0),
+        ("third", 3, 2),
+        ("finish", 0, 4),
         ("place", 0, 0),
-        ("finish", 0, 4),
-        ("finish", 0, 1),
-        ("third", 2, 5),
         ("finish", 0, 3),
         ("place", 0, 3),
+        ("place", 0, 1),
         ("place", 0, 4),
-        ("place", 0, 1),
+        ("finish", 0, 5),
+        ("place", 0, 5),
         ("finish", 0, 2),
         ("place", 0, 2),
-        ("finish", 0, 5),
-        ("place", 0, 5),
     ),
 }
-PAIRED = (1, 2, 2, 2)
+PAIRED = ((5,), (5, 2), (5, 2), (5, 2))
 CHAINED = (True, False, False, False)
 
 
@@ -223,7 +221,6 @@
     gatt,
     qt,
     gat,
-    dkv_out,
     dkv_in,
     gpj_own,
     gpj_oth,
@@ -380,7 +377,7 @@
         cols = pair_cols(head)
         keys = slice(BLOCK * part, BLOCK * part + BLOCK)
         scores = dot_nt(q_own[:, cols] * head_lanes[head % 2], k_row[keys, cols])
-        return jnp.where(key_live[:, keys], scores, -1e30)
+        return jnp.where(key_live[:, keys], scores, -1e30) if part == 1 else scores
 
     gathered = {}
 
@@ -476,7 +473,7 @@
     put_bias(54, col_sum(pulled_low.astype(FULL)))
     own_384 = pl.ds(aligned(blk * 384, 384), 384)
     oth_384 = pl.ds(aligned(oth * 384, 384), 384)
-    core_copies.append(act_copies[0])
+    core_copies.append(None)
     core_copies.append(to_core(4, gred_own.at[:, oth_384], gred_oth))
 
     def send(src, dst, send_sem, recv_sem, dev):
@@ -519,7 +516,7 @@
         grad[chip, unit] = value.astype(LOW)
 
     def paired(plane, unit):
-        return unit >= 6 - PAIRED[plane]
+        return unit in PAIRED[plane]
 
     def kept(plane):
         return (lax.rem(zz, 2) == 0) if plane < 2 else (lax.rem(zz, 2) == 1)
@@ -533,7 +530,7 @@
     def pair_copy(plane, unit):
         return pltpu.make_async_remote_copy(
             src_ref=grad.at[pl.ds(4 * plane, 4), unit],
-            dst_ref=pair_in.at[plane % 2, 5 - unit],
+            dst_ref=pair_in.at[plane % 2, PAIRED[plane].index(unit)],
             send_sem=pair_send.at[plane, unit],
             recv_sem=pair_recv.at[plane, unit],
             device_id=pair_dev,
@@ -626,7 +623,7 @@
 
             @pl.loop(0, 4)
             def _(chip):
-                add_unit(4 * plane + chip, unit, [pair_in[plane % 2, 5 - unit, chip]])
+                add_unit(4 * plane + chip, unit, [pair_in[plane % 2, PAIRED[plane].index(unit), chip]])
 
             for copy in first_copies(plane, unit):
                 copy.start()
@@ -795,15 +792,11 @@
         chip, unit = (at // 6, at % 6) if isinstance(at, int) else (lax.div(at, 6), lax.rem(at, 6))
         grad[chip, unit, rows, :] = values.astype(LOW)
 
-    for copy in act_copies:
-        copy.wait_recv()
-    core_copies[4].wait_recv()
-
-    reduced_both = both(gred_own[:, own_384], gred_oth[...])
-
-    def reduce_rows(first, count, before=0):
-        cols = slice(96 * (first - 64) - before, 96 * (first - 64 + count))
-        part = dot_tn(both(act_own[:, cols], act_oth[:, cols]), reduced_both)
+    def reduce_cols(first, count):
+        before = 96 * (first - 64) % LANES
+        return slice(96 * (first - 64) - before, 96 * (first - 64 + count)), before
+
+    def put_reduced(first, count, before, part):
         for unit in range(count):
             for tile in range(3):
                 put_unit(
@@ -815,15 +808,7 @@
                     ],
                 )
 
-    for third in range(3):
-        for chip in range(12, CHIPS):
-            first = 6 * chip + 2 * third
-            reduce_rows(first, 2, before=96 * (first - 64) % LANES)
-        serve("reduce" + str(third))
-    reduce_rows(64, 8)
-    serve("reduce3")
-
-    for at in range(6):
+    def slope_step(at):
         half = oth if at < 3 else blk
         part_at = at % 3 * 512
         cols = pl.ds(aligned(half * 1536 + part_at, 512), 512)
@@ -835,8 +820,37 @@
             bias_sum[pl.ds(30 + half * 12 + at % 3 * 4 + tile, 1), :] = sums[
                 :, LANES * tile : LANES * tile + LANES
             ]
+
+    reduced_own = gred_own[:, own_384]
+    begun = {}
+    for chip in range(12, CHIPS):
+        cols, _ = reduce_cols(6 * chip, 2)
+        begun[chip] = dot_tn(act_own[:, cols], reduced_own)
+    slope_step(0)
+    for copy in act_copies:
+        copy.wait_recv()
+    core_copies[4].wait_recv()
+    reduced_both = both(reduced_own, gred_oth[...])
+
+    for third in range(3):
+        for chip in range(12, CHIPS):
+            first = 6 * chip + 2 * third
+            cols, before = reduce_cols(first, 2)
+            if third == 0:
+                part = begun[chip] + dot_tn(act_oth[:, cols], gred_oth[...])
+            else:
+                part = dot_tn(both(act_own[:, cols], act_oth[:, cols]), reduced_both)
+            put_reduced(first, 2, before, part)
+        serve("reduce" + str(third))
+    cols, _ = reduce_cols(64, 8)
+    put_reduced(64, 8, 0, dot_tn(both(act_own[:, cols], act_oth[:, cols]), reduced_both))
+    serve("reduce3")
+
+    for at in range(1, 6):
+        slope_step(at)
         if at == 2:
             core_copies.append(to_core(5, gexp_own.at[oth], gexp_oth))
+            serve("slopes0")
 
     serve("slopes")
     grad_mixed = resid_two[...]
@@ -911,23 +925,21 @@
             slope[at : at + HEAD_DIM, slot] = dot_nn(gat[rows, :], soft_low).astype(LOW)
         gpj_own[:, cols] = (grad_query * HEAD_DIM ** (-0.5)).astype(LOW)
 
-    for part in range(3):
-
-        @pl.loop(2 * part, 2 * part + 2)
-        def _(pair):
-            head_pair(pair)
-
-        serve("heads" + str(part))
+    for pair in range(HEADS // 2):
+        head_pair(pair)
+        serve("heads" + str(pair))
 
     def turned(pair, block, first):
         lanes = pl.ds(aligned(pair * ROW + block * BLOCK, BLOCK), BLOCK)
         return slope[first : first + LANES, lanes].T
 
+    for copy in act_copies:
+        copy.wait_send()
     for pair in range(HEADS // 2):
         for first in (0, LANES):
             at = pair * LANES + first * (WIDTH // LANES)
-            dkv_out[:, at : at + LANES] = turned(pair, oth, first)
-    core_copies.append(to_core(7, dkv_out, dkv_in))
+            act_own[:, at : at + LANES] = turned(pair, oth, first)
+    core_copies.append(to_core(7, act_own.at[:, : 2 * WIDTH], dkv_in))
     core_copies[7].wait_recv()
     for pair in range(HEADS // 2):
         for first in (0, LANES):
@@ -946,6 +958,9 @@
         gin_own[...] = (resid_one[...] + dot_nt(gpj_own[...], wp[...])).astype(LOW)
         pltpu.make_async_copy(gin_own, input_gradient, out_sem.at[1]).start()
 
+    input_gradient_part()
+    serve("input")
+
     core_copies[8].wait_recv()
 
     @pl.loop(0, 3, unroll=3)
@@ -963,8 +978,6 @@
                 ])
 
     serve("project")
-    input_gradient_part()
-    serve("input")
 
     serve("end")
 
@@ -988,8 +1001,9 @@
     move_rows(19, 31)
     stores[1].start()
 
-    for copy in core_copies + act_copies[1:]:
-        copy.wait_send()
+    for copy in core_copies:
+        if copy is not None:
+            copy.wait_send()
 
     for plane in range(4):
         for unit in range(6):
@@ -1131,14 +1145,13 @@
         low(WIDTH, BLOCK),
         low(WIDTH, BLOCK),
         low(BLOCK, 2 * WIDTH),
-        low(BLOCK, 2 * WIDTH),
         low(BLOCK, 3 * WIDTH),
         low(BLOCK, 3 * WIDTH // 2),
         full(BLOCK, ROW),
         low(BLOCK, WIDTH),
         low(BLOCK, WIDTH),
         low(CHIPS, 6, UNIT, LANES),
-        low(2, max(PAIRED), 4, UNIT, LANES),
+        low(2, max(map(len, PAIRED)), 4, UNIT, LANES),
         low(4, 6, 2, UNIT, LANES),
         low(4, 6, UNIT, LANES),
         low(24 + 6 * sum(CHAINED), UNIT, LANES),

time: 86.8 us -> 85.3 us (0.983)
  Pallas kernels: 83.2 us -> 81.6 us
    pallas_call x1, Pallas kernels: 80.9 us -> 79.3 us  [fused_layer(): pl.pallas_call(layer_kernel, out_shape=results, in_specs=[anywhere] * 7 +...]
where the time goes in v5:
time: 85.3 us; the launch traced here: 85 us
  Pallas kernels  81.6 us (96%)
  between operations  3.39 us (4%)
    pallas_call x1, Pallas kernels, fused_layer(): pl.pallas_call(layer_kernel, out_shape=results, in_specs=[anywhere] * 7 +...  79.3 us
    pallas_call x1, Pallas kernels, fused_layer(): pl.pallas_call(hand_over, out_shape=results, in_specs=[anywhere] * 3, out...  2.31 us

profile of v5, /device:TPU:1, one launch (start us, length us, event | category | flops | bytes accessed | tf_op | source)
XLA Modules:
  0.0 85.0 jit_solution(18032723897770504482)
XLA Ops:
  3.2 79.3 %encoder_layer.1 = (bf16[256,768]{1,0:T(8,128)(2,1)}, bf16[256,768]{1,0:T(8,128)(2,1)}, f32[1736,128]{1,0:T(8,128)}) custom-call(bf16[256,768]{1,0:T(8,128)(2,1)} %bitcast.8, bf16[256,768]{1,0:T(8,128)(2,1)} %bitcast.9, bf16[12,256,512]{2,1,0:T(8,128)(2,1)} %bitcast.7, bf16[768,2304]{1,0:T(8,128)(2,1)} %w_project.1, bf16[768,768]{1,0:T(8,128)(2,1)} %w_output.1, ...), custom_call_target="tpu_custom_call" | custom-call | tf_op jit(solution)/shard_map/encoder_layer/pallas_call | solution.py:1187
  82.5 2.3 %hand_over.1 = (bf16[256,768]{1,0:T(8,128)(2,1)}, bf16[256,768]{1,0:T(8,128)(2,1)}, f32[1736,128]{1,0:T(8,128)}) custom-call(bf16[256,768]{1,0:T(8,128)(2,1)} %get-tuple-element.9.refs_0_, bf16[256,768]{1,0:T(8,128)(2,1)} %get-tuple-element.10.refs_1_, f32[1736,128]{1,0:T(8,128)} %get-tuple-element.11.refs_2_), custom_call_target="tpu_custom_call" | custom-call | tf_op jit(solution)/shard_map/hand_over/pallas_call | solution.py:1208

commit v6 on v5

--- a/solution.py
+++ b/solution.py
@@ -281,6 +281,22 @@
         load(6 + part, w_project.at[:, part_cols], wp.at[:, part_cols])
         for part, part_cols in enumerate(pl.ds(WIDTH * part, WIDTH) for part in range(3))
     ]
+    barrier = pltpu.get_barrier_semaphore()
+
+    def greet(dev):
+        pl.semaphore_signal(barrier, inc=1, device_id=dev, device_id_type=MESH)
+
+    greet(core_dev)
+    greet(x_dev)
+    greet(y_dev)
+    for step in range(1, 4):
+        greet((lax.rem(dp + 4 * step, CHIPS), blk))
+        greet((lax.rem(dp + 4 * step, CHIPS), oth))
+
+    @pl.when((blk == 1) & (dp < CHIPS - 1))
+    def _():
+        greet((dp + 1, 0))
+
     small = []
     for at, (src, dst) in enumerate(zip(vectors, vector_at)):
         small.append(pltpu.make_async_copy(src, dst.at[0], vector_sem.at[at]))
@@ -299,22 +315,6 @@
         start_vector,
         end_vector,
     ) = vector_at
-
-    barrier = pltpu.get_barrier_semaphore()
-
-    def greet(dev):
-        pl.semaphore_signal(barrier, inc=1, device_id=dev, device_id_type=MESH)
-
-    greet(core_dev)
-    greet(x_dev)
-    greet(y_dev)
-    for step in range(1, 4):
-        greet((lax.rem(dp + 4 * step, CHIPS), blk))
-        greet((lax.rem(dp + 4 * step, CHIPS), oth))
-
-    @pl.when((blk == 1) & (dp < CHIPS - 1))
-    def _():
-        greet((dp + 1, 0))
 
     def to_core(at, src, dst):
         copy = pltpu.make_async_remote_copy(
@@ -510,10 +510,13 @@
         return 4 * plane + 2 * y_at + x_at
 
     def add_unit(chip, unit, arrivals):
-        value = grad[chip, unit].astype(FULL)
-        for arrival in arrivals:
-            value = value + arrival.astype(FULL)
-        grad[chip, unit] = value.astype(LOW)
+        @pl.loop(0, 3)
+        def _(at):
+            rows = pl.ds(aligned(96 * at, 96), 96)
+            value = grad[chip, unit, rows, :].astype(FULL)
+            for arrival in arrivals:
+                value = value + arrival[rows, :].astype(FULL)
+            grad[chip, unit, rows, :] = value.astype(LOW)
 
     def paired(plane, unit):
         return unit in PAIRED[plane]
@@ -623,7 +626,7 @@
 
             @pl.loop(0, 4)
             def _(chip):
-                add_unit(4 * plane + chip, unit, [pair_in[plane % 2, PAIRED[plane].index(unit), chip]])
+                add_unit(4 * plane + chip, unit, [pair_in.at[plane % 2, PAIRED[plane].index(unit), chip]])
 
             for copy in first_copies(plane, unit):
                 copy.start()
@@ -636,7 +639,7 @@
         def step():
             first_copies(plane, unit, (0,))[0].wait_recv()
             _, _, _, behind = crossing(plane, unit)
-            add_unit(behind, unit, [first_in[plane, unit, 0]])
+            add_unit(behind, unit, [first_in.at[plane, unit, 0]])
             second_copy(plane, unit).start()
 
         taking_part(plane, unit, step)
@@ -646,7 +649,7 @@
             first_copies(plane, unit, (1,))[0].wait_recv()
             second_copy(plane, unit).wait_recv()
             add_unit(
-                owner(plane, xx, yy), unit, [first_in[plane, unit, 1], second_in[plane, unit]]
+                owner(plane, xx, yy), unit, [first_in.at[plane, unit, 1], second_in.at[plane, unit]]
             )
             leaves = zz != plane
             if chained(plane, unit):
@@ -667,7 +670,7 @@
         def _():
             slot = passing_slot(plane, unit)
             wait_recv(far_in.at[slot], far_recv.at[slot])
-            add_unit(owner(plane, xx, yy), unit, [far_in[slot]])
+            add_unit(owner(plane, xx, yy), unit, [far_in.at[slot]])
             far_copy(plane, unit).start()
 
     def finish_step(_, unit):

time: 85.3 us -> 85.5 us (level)
  no operation moved by 1% of the time
where the time goes in v6:
time: 85.5 us; the launch traced here: 85.3 us
  Pallas kernels  82 us (96%)
  between operations  3.39 us (4%)
    pallas_call x1, Pallas kernels, fused_layer(): pl.pallas_call(layer_kernel, out_shape=results, in_specs=[anywhere] * 7 +...  79.6 us
    pallas_call x1, Pallas kernels, fused_layer(): pl.pallas_call(hand_over, out_shape=results, in_specs=[anywhere] * 3, out...  2.31 us

profile of v6, /device:TPU:1, one launch (start us, length us, event | category | flops | bytes accessed | tf_op | source)
XLA Modules:
  0.0 85.3 jit_solution(9221699181583891549)
XLA Ops:
  3.2 79.6 %encoder_layer.1 = (bf16[256,768]{1,0:T(8,128)(2,1)}, bf16[256,768]{1,0:T(8,128)(2,1)}, f32[1736,128]{1,0:T(8,128)}) custom-call(bf16[256,768]{1,0:T(8,128)(2,1)} %bitcast.8, bf16[256,768]{1,0:T(8,128)(2,1)} %bitcast.9, bf16[12,256,512]{2,1,0:T(8,128)(2,1)} %bitcast.7, bf16[768,2304]{1,0:T(8,128)(2,1)} %w_project.1, bf16[768,768]{1,0:T(8,128)(2,1)} %w_output.1, ...), custom_call_target="tpu_custom_call" | custom-call | tf_op jit(solution)/shard_map/encoder_layer/pallas_call | solution.py:1190
  82.9 2.3 %hand_over.1 = (bf16[256,768]{1,0:T(8,128)(2,1)}, bf16[256,768]{1,0:T(8,128)(2,1)}, f32[1736,128]{1,0:T(8,128)}) custom-call(bf16[256,768]{1,0:T(8,128)(2,1)} %get-tuple-element.9.refs_0_, bf16[256,768]{1,0:T(8,128)(2,1)} %get-tuple-element.10.refs_1_, f32[1736,128]{1,0:T(8,128)} %get-tuple-element.11.refs_2_), custom_call_target="tpu_custom_call" | custom-call | tf_op jit(solution)/shard_map/hand_over/pallas_call | solution.py:1211
